TPU v7x, 512 devices: a whole 4x4x16 slice. The times are simulated.
512 devices in a mesh: cluster: 16 (over z), sub: 32 (over y, x, core).
Axes of the slice: x: 4, y: 4, z: 16, core: 2. Of those that a mesh axis runs over, the one named last changes fastest.
Arguments:
- features: bfloat16 [196608, 256], P(('cluster', 'sub')), may hold values from -6 to 6
- grad_out: bfloat16 [196608, 256], P(('cluster', 'sub')), may hold values from -6 to 6
- w_self: bfloat16 [256, 256], replicated, may hold values from -0.375 to 0.375
- w_neigh: bfloat16 [256, 256], replicated, may hold values from -0.375 to 0.375
- bias: float32 [256], replicated, may hold values from -3 to 3
- tile_dst: int32 [30720], P(('cluster', 'sub')), may hold values from 0 to 2
- tile_src: int32 [30720], P(('cluster', 'sub')), may hold values from 0 to 50, as said below
- tile_weight: bfloat16 [30720, 128, 128], P(('cluster', 'sub')), may hold values from 0 to 4
- recv_sub: int32 [512, 32], P(('cluster', 'sub')), may hold values from 0 to 1
- recv_cluster: int32 [512, 16], P(('cluster', 'sub')), may hold values from 0 to 1
Outputs:
- grad_features: bfloat16 [196608, 256], P(('cluster', 'sub'))
Inputs may be any that keep to these rules, and one draw needn't show every extreme that they name: `tile_src`: within one partition's 60 tiles, each of the source-table entries 3 to 50 is named by exactly one tile; the other tiles name own blocks.
All inputs are finite; a program needn't handle non-finite values.
Results may differ from a plain program's by a relative error of at most 0.005.
Values may be sent and summed in bfloat16 or wider, within the bound.
A program may use at most 64 MiB of HBM per device.

v0:
```python
import jax
import jax.numpy as jnp
from jax import lax
from jax.sharding import PartitionSpec as P


def gelu_tanh(values):
    return (
        0.5
        * values
        * (1.0 + jnp.tanh(0.7978845608028654 * (values + 0.044715 * values * values * values)))
    )


def shards(
    features,
    grad_out,
    w_self,
    w_neigh,
    bias,
    tile_dst,
    tile_src,
    tile_weight,
    recv_sub,
    recv_cluster,
):
    sub_count = lax.axis_size("sub")
    cluster_count = lax.axis_size("cluster")
    tile_rows = tile_weight.shape[1]
    feature_dim = features.shape[1]
    own_count = features.shape[0] // tile_rows
    source_count = own_count + sub_count + cluster_count
    blocks = features.reshape(own_count, tile_rows, feature_dim)
    sent_sub = lax.all_to_all(
        recv_sub.reshape(sub_count, 1), "sub", split_axis=0, concat_axis=0, tiled=True
    )[:, 0]
    sent_cluster = lax.all_to_all(
        recv_cluster.reshape(cluster_count, 1), "cluster", split_axis=0, concat_axis=0, tiled=True
    )[:, 0]
    halo_sub = lax.all_to_all(blocks[sent_sub], "sub", split_axis=0, concat_axis=0, tiled=True)
    halo_cluster = lax.all_to_all(
        blocks[sent_cluster], "cluster", split_axis=0, concat_axis=0, tiled=True
    )
    source = jnp.concatenate([blocks, halo_sub, halo_cluster], axis=0)
    picked = source[tile_src]
    products = jnp.einsum("tij,tjd->tid", tile_weight, picked, preferred_element_type=jnp.float32)
    own_ids = jnp.arange(own_count, dtype=jnp.int32)
    dst_onehot = (tile_dst[None, :] == own_ids[:, None]).astype(jnp.float32)
    aggregate = jnp.einsum("bt,tid->bid", dst_onehot, products, precision=lax.Precision.HIGHEST)
    row_sums = jnp.sum(tile_weight.astype(jnp.float32), axis=2)
    degree = jnp.dot(dst_onehot, row_sums, precision=lax.Precision.HIGHEST)
    inverse = 1.0 / (degree + 1.0)
    neighbour_mean = (
        (aggregate * inverse[:, :, None])
        .astype(jnp.bfloat16)
        .reshape(own_count * tile_rows, feature_dim)
    )
    pre = jnp.dot(features, w_self, preferred_element_type=jnp.float32)
    pre = pre + jnp.dot(neighbour_mean, w_neigh, preferred_element_type=jnp.float32) + bias
    _, pullback = jax.vjp(gelu_tanh, pre)
    grad_pre = pullback(grad_out.astype(jnp.float32))[0].astype(jnp.bfloat16)
    grad_self = jnp.dot(grad_pre, w_self.T, preferred_element_type=jnp.float32)
    spread = jnp.dot(grad_pre, w_neigh.T, preferred_element_type=jnp.float32).reshape(
        own_count, tile_rows, feature_dim
    )
    spread = (spread * inverse[:, :, None]).astype(jnp.bfloat16)
    returned = jnp.einsum(
        "tij,tid->tjd", tile_weight, spread[tile_dst], preferred_element_type=jnp.float32
    )
    source_ids = jnp.arange(source_count, dtype=jnp.int32)
    src_onehot = (tile_src[None, :] == source_ids[:, None]).astype(jnp.float32)
    partial_value = jnp.einsum("st,tid->sid", src_onehot, returned, precision=lax.Precision.HIGHEST)
    sub_part = partial_value[own_count : own_count + sub_count].astype(jnp.bfloat16)
    cluster_part = partial_value[own_count + sub_count :].astype(jnp.bfloat16)
    back_sub = lax.all_to_all(sub_part, "sub", split_axis=0, concat_axis=0, tiled=True)
    back_cluster = lax.all_to_all(cluster_part, "cluster", split_axis=0, concat_axis=0, tiled=True)
    owner_sub = (sent_sub[None, :] == own_ids[:, None]).astype(jnp.float32)
    owner_cluster = (sent_cluster[None, :] == own_ids[:, None]).astype(jnp.float32)
    back = partial_value[:own_count]
    back = back + jnp.einsum(
        "bp,pid->bid", owner_sub, back_sub.astype(jnp.float32), precision=lax.Precision.HIGHEST
    )
    back = back + jnp.einsum(
        "bp,pid->bid",
        owner_cluster,
        back_cluster.astype(jnp.float32),
        precision=lax.Precision.HIGHEST,
    )
    total = grad_self + back.reshape(own_count * tile_rows, feature_dim)
    return total.astype(jnp.bfloat16)


def solution(mesh):
    placed = (
        P(("cluster", "sub"), None),
        P(("cluster", "sub"), None),
        P(),
        P(),
        P(),
        P(("cluster", "sub")),
        P(("cluster", "sub")),
        P(("cluster", "sub"), None, None),
        P(("cluster", "sub"), None),
        P(("cluster", "sub"), None),
    )
    return jax.shard_map(
        shards, mesh=mesh, in_specs=placed, out_specs=P(("cluster", "sub"), None), check_vma=False
    )
```

profile of v0, /device:TPU:24, one launch (start us, length us, event | category | flops | bytes accessed | tf_op | source)
XLA Modules:
  0.0 287.9 jit_solution(13886912782779376101)
XLA Ops:
  0.0 0.0 copy-start
  0.0 1.4 copy.47
  1.4 9.2 %all-to-all-start = ((s32[32,1,1]{2,1,0:T(1,128)}), s32[32,1,1]{2,1,0:T(1,128)S(1)}, u32[]{:S(2)}, u32[]{:S(2)}) async-start(s32[32,1,1]{2,1,0:T(1,128)} %copy.47), calls=%async_computation | async-start | bytes 32768 | tf_op jit(solution)/shard_map/all_to_all | solution.py:34
  10.6 1.3 copy.48
  11.9 4.0 %all-to-all-done = s32[32,1,1]{2,1,0:T(1,128)S(1)} async-done(((s32[32,1,1]{2,1,0:T(1,128)}), s32[32,1,1]{2,1,0:T(1,128)S(1)}, u32[]{:S(2)}, u32[]{:S(2)}) %all-to-all-start) | async-done | bytes 160 | tf_op jit(solution)/shard_map/all_to_all | solution.py:34
  16.0 13.4 %all-to-all-start.2 = ((s32[16,1,1]{2,1,0:T(1,128)}), s32[16,1,1]{2,1,0:T(1,128)S(1)}, u32[]{:S(2)}, u32[]{:S(2)}) async-start(s32[16,1,1]{2,1,0:T(1,128)} %copy.48), calls=%async_computation.2 | async-start | bytes 16384 | tf_op jit(solution)/shard_map/all_to_all | solution.py:37
  29.3 0.7 reduce
  30.0 0.0 copy-start.2
  30.0 3.0 %gather_fusion = bf16[32,128,256]{2,1,0:T(8,128)(2,1)} fusion(bf16[3,128,256]{2,1,0:T(8,128)(2,1)} %bitcast.47, s32[1024]{0:T(1024)S(1)} %pad_clamp_fusion.3), kind=kCustom, calls=%fused_computation | custom fusion | bytes 4194432 | tf_op jit(solution)/shard_map/gather | solution.py:40
  33.0 0.0 copy-start.8
  33.0 0.0 copy-start.9
  33.0 0.0 copy-start.3
  33.0 8.7 %all-to-all-done.2 = s32[16,1,1]{2,1,0:T(1,128)S(1)} async-done(((s32[16,1,1]{2,1,0:T(1,128)}), s32[16,1,1]{2,1,0:T(1,128)S(1)}, u32[]{:S(2)}, u32[]{:S(2)}) %all-to-all-start.2) | async-done | bytes 96 | tf_op jit(solution)/shard_map/all_to_all | solution.py:37
  41.8 6.6 %all-to-all-start.1 = ((bf16[32,128,256]{2,1,0:T(8,128)(2,1)}), bf16[32,128,256]{2,1,0:T(8,128)(2,1)}, u32[]{:S(2)}, u32[]{:S(2)}) async-start(bf16[32,128,256]{2,1,0:T(8,128)(2,1)} %gather_fusion), calls=%async_computation.1 | async-start | bytes 4194304 | tf_op jit(solution)/shard_map/all_to_all | solution.py:40
  48.4 0.0 copy-start.5
  48.4 0.4 reduce.1
  48.8 0.0 copy-done.2
  48.8 1.6 gather_fusion.1
  50.4 25.2 %all-to-all-done.1 = bf16[32,128,256]{2,1,0:T(8,128)(2,1)} async-done(((bf16[32,128,256]{2,1,0:T(8,128)(2,1)}), bf16[32,128,256]{2,1,0:T(8,128)(2,1)}, u32[]{:S(2)}, u32[]{:S(2)}) %all-to-all-start.1) | async-done | bytes 2097184 | tf_op jit(solution)/shard_map/all_to_all | solution.py:40
  75.6 3.7 %all-to-all-start.3 = ((bf16[16,128,256]{2,1,0:T(8,128)(2,1)}), bf16[16,128,256]{2,1,0:T(8,128)(2,1)S(1)}, u32[]{:S(2)}, u32[]{:S(2)}) async-start(bf16[16,128,256]{2,1,0:T(8,128)(2,1)} %gather_fusion.1), calls=%async_computation.3 | async-start | bytes 2097152 | tf_op jit(solution)/shard_map/all_to_all | solution.py:41
  79.3 0.0 copy-done.8
  79.3 0.0 copy-done.9
  79.3 0.0 copy-done.3
  79.3 0.6 convert_reduce_fusion
  79.9 0.1 fusion.10
  80.1 0.0 copy-done.5
  80.1 1.0 fusion.41
  81.1 47.1 %all-to-all-done.3 = bf16[16,128,256]{2,1,0:T(8,128)(2,1)S(1)} async-done(((bf16[16,128,256]{2,1,0:T(8,128)(2,1)}), bf16[16,128,256]{2,1,0:T(8,128)(2,1)S(1)}, u32[]{:S(2)}, u32[]{:S(2)}) %all-to-all-start.3) | async-done | bytes 1048608 | tf_op jit(solution)/shard_map/all_to_all | solution.py:41
  128.2 3.1 %pad_maximum_fusion = bf16[51,128,256]{2,1,0:T(8,128)(2,1)} fusion(bf16[16,128,256]{2,1,0:T(8,128)(2,1)S(1)} %all-to-all-done.3, bf16[32,128,256]{2,1,0:T(8,128)(2,1)} %all-to-all-done.1, bf16[3,128,256]{2,1,0:T(8,128)(2,1)S(1)} %bitcast.49), kind=kLoop, calls=%fused_computation.5 | loop fusion | flops 3342336 | bytes 6684672 | tf_op jit(solution)/shard_map/concatenate | solution.py:44
  131.3 4.6 %gather_fusion.2 = bf16[60,128,256]{2,1,0:T(8,128)(2,1)} fusion(bf16[51,128,256]{2,1,0:T(8,128)(2,1)} %pad_maximum_fusion, s32[1024]{0:T(1024)S(1)} %pad_clamp_fusion.1), kind=kCustom, calls=%fused_computation.2 | custom fusion | bytes 7864560 | tf_op jit(solution)/shard_map/gather | solution.py:45
  136.0 6.4 %convolution_bitcast_fusion.1 = f32[60,128,256]{1,2,0:T(8,128)} fusion(bf16[60,128,256]{2,1,0:T(8,128)(2,1)} %gather_fusion.2, bf16[60,128,128]{2,1,0:T(8,128)(2,1)S(1)} %copy-done.3), kind=kOutput, calls=%fused_computation.7 | convolution fusion | flops 503316480 | bytes 13762560 | tf_op jit(solution)/shard_map/tij,tjd->tid/dot_general | solution.py:46
  142.4 9.0 %copy.50 = f32[60,128,256]{2,0,1:T(8,128)} copy(f32[60,128,256]{1,2,0:T(8,128)} %convolution_bitcast_fusion.1) | data formatting | bytes 15728640 | tf_op jit(solution)/shard_map/tij,tjd->tid/dot_general | solution.py:46
  151.4 0.0 copy-start.7
  151.4 0.0 copy-start.10
  151.4 6.2 %fusion.28 = f32[3,128,256]{2,0,1:T(4,128)S(1)} fusion(f32[60,128,256]{2,0,1:T(8,128)} %copy.50, s32[60]{0:T(128)S(1)} %copy-done.8), kind=kOutput, calls=%fused_computation.54 | convolution fusion | flops 70779056 | bytes 8257776 | tf_op jit(solution)/shard_map/bt,tid->bid/dot_general | solution.py:49
  157.6 0.1 fusion.22
  157.8 0.0 copy-done
  157.8 0.0 copy-done.7
  157.8 0.0 copy-done.10
  157.8 0.0 copy-done.11
  157.8 0.5 fusion.17
  158.3 0.2 fusion.42
  158.6 0.1 multiply_convert_fusion
  158.7 2.7 gather_fusion.3
  161.4 6.4 %convolution_bitcast_fusion = f32[60,128,256]{1,2,0:T(8,128)} fusion(bf16[60,128,256]{2,1,0:T(8,128)(2,1)} %gather_fusion.3, bf16[60,128,128]{2,1,0:T(8,128)(2,1)S(1)} %copy-done.3), kind=kOutput, calls=%fused_computation.6 | convolution fusion | flops 503316480 | bytes 13762560 | tf_op jit(solution)/shard_map/tij,tid->tjd/dot_general | solution.py:67
  167.8 9.0 %copy.53 = f32[60,128,256]{2,0,1:T(8,128)} copy(f32[60,128,256]{1,2,0:T(8,128)} %convolution_bitcast_fusion) | data formatting | bytes 15728640 | tf_op jit(solution)/shard_map/tij,tid->tjd/dot_general | solution.py:67
  176.8 10.9 %fusion.40 = (bf16[51,128,256]{2,0,1:T(8,128)(2,1)S(1)}, f32[51,128,256]{2,0,1:T(8,128)}) fusion(f32[60,128,256]{2,0,1:T(8,128)} %copy.53, s32[60]{0:T(128)S(1)} %copy-done.9), kind=kOutput, calls=%fused_computation.63 | convolution fusion | flops 1204915200 | bytes 17891568 | tf_op jit(solution)/shard_map/st,tid->sid/dot_general | solution.py:72
  187.8 1.8 copy-done.4
  189.5 0.5 slice.24
  190.1 1.3 copy.56
  191.4 7.9 %all-to-all-start.5 = ((bf16[16,128,256]{2,1,0:T(8,128)(2,1)}), bf16[16,128,256]{2,1,0:T(8,128)(2,1)S(1)}, u32[]{:S(2)}, u32[]{:S(2)}) async-start(bf16[16,128,256]{2,1,0:T(8,128)(2,1)} %copy.56), calls=%async_computation.5 | async-start | bytes 2097152 | tf_op jit(solution)/shard_map/all_to_all | solution.py:76
  199.3 2.9 %slice.23 = bf16[32,128,256]{2,0,1:T(8,128)(2,1)S(1)} slice(bf16[51,128,256]{2,0,1:T(8,128)(2,1)} %copy-done.4), slice={[3:35], [0:128], [0:256]} | slice | bytes 4194304 | tf_op jit(solution)/shard_map/slice | solution.py:73
  202.2 2.5 copy.54
  204.8 44.7 %all-to-all-done.5 = bf16[16,128,256]{2,1,0:T(8,128)(2,1)S(1)} async-done(((bf16[16,128,256]{2,1,0:T(8,128)(2,1)}), bf16[16,128,256]{2,1,0:T(8,128)(2,1)S(1)}, u32[]{:S(2)}, u32[]{:S(2)}) %all-to-all-start.5) | async-done | bytes 1048608 | tf_op jit(solution)/shard_map/all_to_all | solution.py:76
  249.4 7.5 %all-to-all-start.4 = ((bf16[32,128,256]{2,1,0:T(8,128)(2,1)}), bf16[32,128,256]{2,1,0:T(8,128)(2,1)S(1)}, u32[]{:S(2)}, u32[]{:S(2)}) async-start(bf16[32,128,256]{2,1,0:T(8,128)(2,1)} %copy.54), calls=%async_computation.4 | async-start | bytes 4194304 | tf_op jit(solution)/shard_map/all_to_all | solution.py:75
  256.9 0.0 copy-start.1
  256.9 1.5 fusion.11
  258.4 0.0 copy-start.6
  258.4 25.7 %all-to-all-done.4 = bf16[32,128,256]{2,1,0:T(8,128)(2,1)S(1)} async-done(((bf16[32,128,256]{2,1,0:T(8,128)(2,1)}), bf16[32,128,256]{2,1,0:T(8,128)(2,1)S(1)}, u32[]{:S(2)}, u32[]{:S(2)}) %all-to-all-start.4) | async-done | bytes 2097184 | tf_op jit(solution)/shard_map/all_to_all | solution.py:75
  284.2 2.7 fusion.5
  286.8 0.1 copy.58
  286.9 0.0 copy-done.6
  286.9 0.9 fusion.9
  287.9 0.0 copy-done.1
  (10 shorter events, 0.1 us)
Async XLA Ops:
  0.0 157.8 %copy-start = (bf16[256,256]{1,0:T(8,128)(2,1)S(1)}, bf16[256,256]{1,0:T(8,128)(2,1)}, u32[]{:S(2)}) copy-start(bf16[256,256]{1,0:T(8,128)(2,1)} %param.13) | copy-start | bytes 393220
  1.4 14.6 %all-to-all-start = ((s32[32,1,1]{2,1,0:T(1,128)}), s32[32,1,1]{2,1,0:T(1,128)S(1)}, u32[]{:S(2)}, u32[]{:S(2)}) async-start(s32[32,1,1]{2,1,0:T(1,128)} %copy.47), calls=%async_computation | async-start | bytes 32768 | tf_op jit(solution)/shard_map/all_to_all | solution.py:34
  16.0 25.8 %all-to-all-start.2 = ((s32[16,1,1]{2,1,0:T(1,128)}), s32[16,1,1]{2,1,0:T(1,128)S(1)}, u32[]{:S(2)}, u32[]{:S(2)}) async-start(s32[16,1,1]{2,1,0:T(1,128)} %copy.48), calls=%async_computation.2 | async-start | bytes 16384 | tf_op jit(solution)/shard_map/all_to_all | solution.py:37
  30.0 18.8 %copy-start.2 = (bf16[384,256]{1,0:T(8,128)(2,1)S(1)}, bf16[384,256]{1,0:T(8,128)(2,1)}, u32[]{:S(2)}) copy-start(bf16[384,256]{1,0:T(8,128)(2,1)} %param.10) | copy-start | bytes 589828
  33.0 46.2 %copy-start.8 = (s32[60]{0:T(128)S(1)}, s32[60]{0:T(128)}, u32[]{:S(2)}) copy-start(s32[60]{0:T(128)} %param.15) | copy-start | bytes 724
  33.0 46.3 %copy-start.9 = (s32[60]{0:T(128)S(1)}, s32[60]{0:T(128)}, u32[]{:S(2)}) copy-start(s32[60]{0:T(128)} %param.16) | copy-start | bytes 724
  33.0 46.3 %copy-start.3 = (bf16[60,128,128]{2,1,0:T(8,128)(2,1)S(1)}, bf16[60,128,128]{2,1,0:T(8,128)(2,1)}, u32[]{:S(2)}) copy-start(bf16[60,128,128]{2,1,0:T(8,128)(2,1)} %param.17) | copy-start | bytes 5898244
  41.8 33.8 %all-to-all-start.1 = ((bf16[32,128,256]{2,1,0:T(8,128)(2,1)}), bf16[32,128,256]{2,1,0:T(8,128)(2,1)}, u32[]{:S(2)}, u32[]{:S(2)}) async-start(bf16[32,128,256]{2,1,0:T(8,128)(2,1)} %gather_fusion), calls=%async_computation.1 | async-start | bytes 4194304 | tf_op jit(solution)/shard_map/all_to_all | solution.py:40
  48.4 31.7 %copy-start.5 = (bf16[256,256]{1,0:T(8,128)(2,1)S(1)}, bf16[256,256]{1,0:T(8,128)(2,1)}, u32[]{:S(2)}) copy-start(bf16[256,256]{1,0:T(8,128)(2,1)} %param.12) | copy-start | bytes 393220
  75.6 52.6 %all-to-all-start.3 = ((bf16[16,128,256]{2,1,0:T(8,128)(2,1)}), bf16[16,128,256]{2,1,0:T(8,128)(2,1)S(1)}, u32[]{:S(2)}, u32[]{:S(2)}) async-start(bf16[16,128,256]{2,1,0:T(8,128)(2,1)} %gather_fusion.1), calls=%async_computation.3 | async-start | bytes 2097152 | tf_op jit(solution)/shard_map/all_to_all | solution.py:41
  151.4 6.4 %copy-start.7 = (f32[384,256]{1,0:T(8,128)S(1)}, f32[384,256]{1,0:T(8,128)}, u32[]{:S(2)}) copy-start(f32[384,256]{1,0:T(8,128)} %fusion.41) | copy-start | bytes 1179652
  151.4 6.4 %copy-start.10 = (bf16[384,256]{1,0:T(8,128)(2,1)S(1)}, bf16[384,256]{1,0:T(8,128)(2,1)}, u32[]{:S(2)}) copy-start(bf16[384,256]{1,0:T(8,128)(2,1)} %param.11) | copy-start | bytes 589828
  151.4 6.4 %copy-start.11 = (f32[256]{0:T(256)S(1)}, f32[256]{0:T(256)}, u32[]{:S(2)}) copy-start(f32[256]{0:T(256)} %param.14) | copy-start | bytes 3076
  187.7 1.8 copy-start.4
  191.4 58.0 %all-to-all-start.5 = ((bf16[16,128,256]{2,1,0:T(8,128)(2,1)}), bf16[16,128,256]{2,1,0:T(8,128)(2,1)S(1)}, u32[]{:S(2)}, u32[]{:S(2)}) async-start(bf16[16,128,256]{2,1,0:T(8,128)(2,1)} %copy.56), calls=%async_computation.5 | async-start | bytes 2097152 | tf_op jit(solution)/shard_map/all_to_all | solution.py:76
  249.4 34.7 %all-to-all-start.4 = ((bf16[32,128,256]{2,1,0:T(8,128)(2,1)}), bf16[32,128,256]{2,1,0:T(8,128)(2,1)S(1)}, u32[]{:S(2)}, u32[]{:S(2)}) async-start(bf16[32,128,256]{2,1,0:T(8,128)(2,1)} %copy.54), calls=%async_computation.4 | async-start | bytes 4194304 | tf_op jit(solution)/shard_map/all_to_all | solution.py:75
  256.9 30.9 %copy-start.1 = (bf16[256,256]{1,0:T(8,128)(2,1)S(1)}, bf16[256,256]{1,0:T(8,128)(2,1)}, u32[]{:S(2)}) copy-start(bf16[256,256]{1,0:T(8,128)(2,1)} %param.13) | copy-start | bytes 393220
  258.4 28.5 %copy-start.6 = (bf16[256,256]{1,0:T(8,128)(2,1)S(1)}, bf16[256,256]{1,0:T(8,128)(2,1)}, u32[]{:S(2)}) copy-start(bf16[256,256]{1,0:T(8,128)(2,1)} %param.12) | copy-start | bytes 393220
where the time goes:
time: 291 us; the launch traced here: 288 us
  waiting for transfers between devices  156 us (54%)
  starting transfers between devices  48.2 us (17%)
  local copies, waits for them, and re-layouts  41.9 us (14%)
  matrix products  36.9 us (13%)
  other arithmetic  5.04 us (2%)
    all_to_all x1, waiting for transfers between devices, shards(): lax.all_to_all(blocks[sent_cluster], 'cluster', split_axis=0, concat_axis...  47.1 us
    all_to_all x1, waiting for transfers between devices, shards(): lax.all_to_all(cluster_part, 'cluster', split_axis=0, concat_axis=0, tile...  44.7 us
    all_to_all x1, waiting for transfers between devices, shards(): lax.all_to_all(sub_part, 'sub', split_axis=0, concat_axis=0, tiled=True)  25.7 us
    all_to_all x1, waiting for transfers between devices, shards(): lax.all_to_all(blocks[sent_sub], 'sub', split_axis=0, concat_axis=0, tile...  25.2 us
    all_to_all x1, starting transfers between devices, shards(): lax.all_to_all(recv_cluster.reshape(cluster_count, 1), 'cluster', split_a...  13.4 us
    dot_general x1, matrix products, shards(): jnp.einsum('st,tid->sid', src_onehot, returned, precision=lax.Precision.H...  10.9 us
    all_to_all x1, starting transfers between devices, shards(): lax.all_to_all(recv_sub.reshape(sub_count, 1), 'sub', split_axis=0, conca...  9.23 us
    dot_general x1, local copies, waits for them, and re-layouts, shards(): jnp.einsum('tij,tid->tjd', tile_weight, spread[tile_dst], preferred_eleme...  9.03 us
  transfers between devices with their start and end apart: 6, of which 6 were waited for; matrix products, arithmetic and copies ran while one was open for 5% of the time, Pallas kernels for 0%

commit v1 on v0

v1 whole, which is shorter than its diff:
```python
import functools

import jax
import jax.numpy as jnp
from jax import lax
from jax.experimental import pallas as pl
from jax.experimental.pallas import tpu as pltpu
from jax.sharding import PartitionSpec as P

MESH = pl.DeviceIdType.MESH
BF = jnp.bfloat16
F32 = jnp.float32
NZ = 16
RING = 4
HALF = NZ // 2
BLK = 128
D = 256
OWN = 3
TILES = 60
N_SUB = 32
REMOTE = N_SUB + NZ
LOCAL = TILES - REMOTE


def wrap(value, size):
    return lax.rem(value + size, size)


def dot_nt(left, right):
    return lax.dot_general(left, right, (((1,), (1,)), ((), ())), preferred_element_type=F32)


def kernel(
    src_ref, dst_ref, rsub_ref, rclu_ref,
    feat, gout, ws, wn, bias, tiles_hbm,
    out,
    w, wt, tab, acc, deg, pre, inv, spread, gself,
    zu, zd, gs, gb,
    pu, pd, su, sd, ru, rd,
    sb, rb, sbp, sbh, rbp, rbh, sap, sah, rap, rah,
    w_sem,
    zu_s, zu_r, zd_s, zd_r, a_s, a_r, b_s, b_r, x_s, x_r,
    ku_s, ku_r, kd_s, kd_r, ka_s, ka_r, kb_s, kb_r, kx_s, kx_r,
):
    c = lax.axis_index("cluster")
    s = lax.axis_index("sub")
    core = lax.rem(s, 2)
    x = lax.rem(s // 2, RING)
    y = s // (2 * RING)
    a = x * (1 - core) + y * core
    b = y * (1 - core) + x * core

    def at(da, db, which):
        aa = wrap(a + da, RING)
        bb = wrap(b + db, RING)
        xx = aa * (1 - core) + bb * core
        yy = bb * (1 - core) + aa * core
        return (yy * RING + xx) * 2 + which

    up = (wrap(c + 1, NZ), s)
    dn = (wrap(c - 1, NZ), s)
    ap = (c, at(1, 0, core))
    am = (c, at(-1, 0, core))
    bp = (c, at(0, 1, core))
    bm = (c, at(0, -1, core))
    sib = (c, at(0, 0, 1 - core))

    def copy(source, target, send, recv, device):
        return pltpu.make_async_remote_copy(
            src_ref=source, dst_ref=target, send_sem=send, recv_sem=recv,
            device_id=device, device_id_type=MESH,
        )

    def same_index(da, db):
        return at(-da, -db, core)

    def other_index(da, db):
        return at(-db, -da, 1 - core)

    load = pltpu.make_async_copy(tiles_hbm, w, w_sem)
    load.start()
    barrier = pltpu.get_barrier_semaphore()
    for device in (up, dn, ap, am, bp, bm, sib):
        pl.semaphore_signal(barrier, inc=1, device_id=device, device_id_type=MESH)
    gs[0, 0] = feat[0:2]
    acc[...] = jnp.zeros_like(acc)
    deg[...] = jnp.zeros_like(deg)
    pl.semaphore_wait(barrier, 7)

    def zu_copy(d, h):
        source = feat.at[h] if d == 1 else zu.at[d - 2, h]
        return copy(source, zu.at[d - 1, h], zu_s.at[d - 1, h], zu_r.at[d - 1, h], up)

    def zd_copy(d, h):
        source = feat.at[h] if d == 1 else zd.at[d - 2, h]
        return copy(source, zd.at[d - 1, h], zd_s.at[d - 1, h], zd_r.at[d - 1, h], dn)

    def has_up(d, h):
        return d < HALF or (d == HALF and h == 0)

    def has_dn(d, h):
        return d < HALF or (d == HALF and h == 1)

    def a_copy(k):
        source, target, device = (
            (gs.at[0, 0], gs.at[1, 0], ap),
            (gs.at[0, 0], gs.at[3, 0], am),
            (gs.at[1, 0, 0], gs.at[2, 0, 0], ap),
            (gs.at[3, 0, 1], gs.at[2, 0, 1], am),
        )[k]
        return copy(source, target, a_s.at[k], a_r.at[k], device)

    def b_copy(da, k):
        source, target, device = (
            (gs.at[da, 0], gs.at[da, 1], bp),
            (gs.at[da, 0], gs.at[da, 3], bm),
            (gs.at[da, 1, 0], gs.at[da, 2, 0], bp),
            (gs.at[da, 3, 1], gs.at[da, 2, 1], bm),
        )[k]
        return copy(source, target, b_s.at[da, k], b_r.at[da, k], device)

    def x_copy(da, db):
        return copy(gs.at[da, db], gb.at[da, db], x_s.at[da, db], x_r.at[da, db], sib)

    def z_start():
        for h in (0, 1):
            zu_copy(1, h).start()
            zd_copy(1, 1 - h).start()

    def z_step(d, h):
        if has_up(d, h):
            zu_copy(d, h).wait_recv()
            if has_up(d + 1, h):
                zu_copy(d + 1, h).start()
        if has_dn(d, 1 - h):
            zd_copy(d, 1 - h).wait_recv()
            if has_dn(d + 1, 1 - h):
                zd_copy(d + 1, 1 - h).start()

    def a_start():
        a_copy(0).start()
        a_copy(1).start()

    def a_mid():
        a_copy(0).wait_recv()
        a_copy(2).start()
        a_copy(1).wait_recv()
        a_copy(3).start()
        for da in (1, 3):
            b_start(da)
            x_copy(da, 0).start()

    def a_end():
        a_copy(2).wait_recv()
        a_copy(3).wait_recv()
        b_start(2)
        x_copy(2, 0).start()

    def b_start(da):
        b_copy(da, 0).start()
        b_copy(da, 1).start()

    def b_mid(da):
        b_copy(da, 0).wait_recv()
        b_copy(da, 2).start()
        b_copy(da, 1).wait_recv()
        b_copy(da, 3).start()
        x_copy(da, 1).start()
        x_copy(da, 3).start()

    def b_end(da):
        b_copy(da, 2).wait_recv()
        b_copy(da, 3).wait_recv()
        x_copy(da, 2).start()

    def find_remote(first, count):
        def body(i, _):
            terms = [jnp.where(src_ref[t] == i + OWN, t, 0) for t in range(TILES)]
            while len(terms) > 1:
                terms = [sum(terms[k : k + 2]) for k in range(0, len(terms), 2)]
            tab[i] = terms[0]
            return 0

        lax.fori_loop(first, first + count, body, 0)

    def find_local():
        def body(t, carry):
            seen, found = carry
            local = src_ref[t] < OWN
            found = tuple(
                jnp.where(jnp.logical_and(local, seen == k), t, found[k]) for k in range(LOCAL)
            )
            return seen + jnp.where(local, 1, 0), found

        zero = jnp.int32(0)
        _, found = lax.fori_loop(0, TILES, body, (zero, (zero,) * LOCAL))
        for k in range(LOCAL):
            tab[REMOTE + k] = found[k]

    def transpose_tiles(first, count):
        def body(t, _):
            wt[t] = w[t].T
            return 0

        lax.fori_loop(first, first + count, body, 0)

    def accumulate(i0, block0, i1, block1):
        rows = []
        t0, t1 = tab[i0], tab[i1]
        w0, w1 = w[t0], w[t1]
        d0, d1 = dst_ref[t0], dst_ref[t1]
        zero = jnp.zeros((BLK, BLK), BF)
        for k in range(OWN):
            rows.append(
                jnp.concatenate([jnp.where(d0 == k, w0, zero), jnp.where(d1 == k, w1, zero)], axis=1)
            )
        left = jnp.concatenate(rows, axis=0)
        right = jnp.concatenate([block0, block1], axis=0)
        acc[...] += jnp.dot(left, right, preferred_element_type=F32)
        deg[...] += jnp.dot(left, jnp.ones((2 * BLK, BLK), BF), preferred_element_type=F32)

    def z_pair(d):
        r0, r1 = wrap(c - d, NZ), wrap(c + d, NZ)
        block0 = jnp.where(rclu_ref[0, r0] == 0, zu[d - 1, 0], zu[d - 1, 1])
        block1 = jnp.where(rclu_ref[0, r1] == 0, zd[d - 1, 0], zd[d - 1, 1])
        accumulate(N_SUB + r0, block0, N_SUB + r1, block1)

    def z_last():
        r0 = wrap(c + HALF, NZ)
        block0 = jnp.where(rclu_ref[0, r0] == 0, zu[HALF - 1, 0], zd[HALF - 1, 1])
        block1 = jnp.where(rclu_ref[0, c] == 0, feat[0], feat[1])
        accumulate(N_SUB + r0, block0, N_SUB + c, block1)

    def sub_pairs(da):
        def body(db, _):
            x_copy(da, db).wait_recv()
            p0, p1 = same_index(da, db), other_index(da, db)
            block0 = jnp.where(rsub_ref[0, p0] == 0, gs[da, db, 0], gs[da, db, 1])
            block1 = jnp.where(rsub_ref[0, p1] == 0, gb[da, db, 0], gb[da, db, 1])
            accumulate(p0, block0, p1, block1)
            return 0

        lax.fori_loop(0, RING, body, 0)

    def local_pairs():
        def body(k, _):
            i0 = REMOTE + 2 * k
            i1 = i0 + 1
            accumulate(i0, feat[src_ref[tab[i0]]], i1, feat[src_ref[tab[i1]]])
            return 0

        lax.fori_loop(0, LOCAL // 2, body, 0)

    def self_product():
        rows = feat[...].reshape(OWN * BLK, D)
        pre[...] = jnp.dot(rows, ws[...], preferred_element_type=F32) + bias[...]

    z_start()
    a_start()
    b_start(0)
    x_copy(0, 0).start()
    self_product()
    load.wait()
    find_local()

    z_step(1, 0)
    find_remote(N_SUB, NZ // 2)
    z_step(1, 1)
    a_mid()
    b_mid(0)
    find_remote(N_SUB + NZ // 2, NZ // 2)

    z_step(2, 0)
    z_pair(1)
    z_step(2, 1)
    a_end()
    b_mid(1)
    b_mid(3)
    b_end(0)
    find_remote(0, 8)

    z_step(3, 0)
    z_pair(2)
    find_remote(8, 8)
    z_step(3, 1)
    b_mid(2)
    b_end(1)
    b_end(3)
    find_remote(16, 8)

    z_step(4, 0)
    z_pair(3)
    find_remote(24, 8)
    z_step(4, 1)
    b_end(2)
    transpose_tiles(0, 20)

    z_step(5, 0)
    z_pair(4)
    transpose_tiles(20, 20)
    z_step(5, 1)
    sub_pairs(0)

    z_step(6, 0)
    z_pair(5)
    transpose_tiles(40, 20)
    z_step(6, 1)
    sub_pairs(1)

    z_step(7, 0)
    z_pair(6)
    sub_pairs(3)
    z_step(7, 1)
    z_pair(7)
    sub_pairs(2)
    local_pairs()
    z_step(8, 0)
    z_last()

    scale = 1.0 / (deg[...] + 1.0)
    inv[...] = jnp.concatenate([scale, scale], axis=1)
    mean = (acc[...] * inv[...]).astype(BF)
    v = pre[...] + jnp.dot(mean, wn[...], preferred_element_type=F32)
    k0, k1 = 0.7978845608028654, 0.044715
    square = v * v
    th = jnp.tanh(k0 * v * (1.0 + k1 * square))
    slope = 0.5 * (1.0 + th) + 0.5 * v * (1.0 - th * th) * (k0 * (1.0 + 3.0 * k1 * square))
    grad_pre = (gout[...].astype(F32) * slope).astype(BF)
    spread[...] = (dot_nt(grad_pre, wn[...]) * inv[...]).astype(BF).reshape(OWN, BLK, D)

    def partial(i):
        t = tab[i]
        return jnp.dot(wt[t], spread[dst_ref[t]], preferred_element_type=F32)

    def only(keep, value):
        return jnp.where(keep, value, jnp.zeros_like(value))

    def ku_copy(d, h):
        return copy(su.at[d - 1, h], ru.at[d - 1, h], ku_s.at[d - 1, h], ku_r.at[d - 1, h], up)

    def kd_copy(d, h):
        return copy(sd.at[d - 1, h], rd.at[d - 1, h], kd_s.at[d - 1, h], kd_r.at[d - 1, h], dn)

    def ku_send(d, h):
        value = only(rclu_ref[0, wrap(c + d, NZ)] == h, pu[d - 1])
        if has_up(d + 1, h):
            ku_copy(d + 1, h).wait_recv()
            value = value + ru[d, h].astype(F32)
        su[d - 1, h] = value.astype(BF)
        ku_copy(d, h).start()

    def kd_send(d, h):
        value = only(rclu_ref[0, wrap(c - d, NZ)] == h, pd[d - 1])
        if has_dn(d + 1, h):
            kd_copy(d + 1, h).wait_recv()
            value = value + rd[d, h].astype(F32)
        sd[d - 1, h] = value.astype(BF)
        kd_copy(d, h).start()

    def z_partials(d):
        pu[d - 1] = partial(N_SUB + wrap(c + d, NZ))
        pd[d - 1] = partial(N_SUB + wrap(c - d, NZ))

    def kx_copy(da, db):
        return copy(sb.at[da, db], rb.at[da, db], kx_s.at[da, db], kx_r.at[da, db], sib)

    def x_send(da):
        def body(db, _):
            p = other_index(da, db)
            value = partial(p)
            for h in (0, 1):
                sb[da, db, h] = only(rsub_ref[0, p] == h, value).astype(BF)
            kx_copy(da, db).start()
            return 0

        lax.fori_loop(0, RING, body, 0)

    def kb_copy(da, k):
        source, target, device = (
            (sbp.at[da, 0], rbp.at[da, 0], bm),
            (sbp.at[da, 1], rbp.at[da, 1], bp),
            (sbh.at[da, 0], rbh.at[da, 0], bm),
            (sbh.at[da, 1], rbh.at[da, 1], bp),
        )[k]
        return copy(source, target, kb_s.at[da, k], kb_r.at[da, k], device)

    def ka_copy(k):
        source, target, device = (
            (sap.at[0], rap.at[0], am),
            (sap.at[1], rap.at[1], ap),
            (sah.at[0], rah.at[0], am),
            (sah.at[1], rah.at[1], ap),
        )[k]
        return copy(source, target, ka_s.at[k], ka_r.at[k], device)

    def chip_sum(da, db):
        p = same_index(da, db)
        value = partial(p)
        kx_copy(da, db).wait_recv()
        return [
            only(rsub_ref[0, p] == h, value) + rb[da, db, h].astype(F32) for h in (0, 1)
        ]

    def b_far(da):
        v0, v1 = chip_sum(da, 2)
        sbh[da, 0] = v0.astype(BF)
        kb_copy(da, 2).start()
        sbh[da, 1] = v1.astype(BF)
        kb_copy(da, 3).start()

    def b_near(da):
        v0, v1 = chip_sum(da, 1)
        sbp[da, 0, 1] = v1.astype(BF)
        kb_copy(da, 2).wait_recv()
        sbp[da, 0, 0] = (v0 + rbh[da, 0].astype(F32)).astype(BF)
        kb_copy(da, 0).start()
        v0, v1 = chip_sum(da, 3)
        sbp[da, 1, 0] = v0.astype(BF)
        kb_copy(da, 3).wait_recv()
        sbp[da, 1, 1] = (v1 + rbh[da, 1].astype(F32)).astype(BF)
        kb_copy(da, 1).start()

    def row_sum(da):
        v = chip_sum(da, 0)
        kb_copy(da, 0).wait_recv()
        kb_copy(da, 1).wait_recv()
        return [v[h] + rbp[da, 0, h].astype(F32) + rbp[da, 1, h].astype(F32) for h in (0, 1)]

    def a_far():
        v = row_sum(2)
        sah[0] = v[0].astype(BF)
        ka_copy(2).start()
        sah[1] = v[1].astype(BF)
        ka_copy(3).start()

    def a_near():
        v = row_sum(1)
        ka_copy(2).wait_recv()
        sap[0, 0] = (v[0] + rah[0].astype(F32)).astype(BF)
        sap[0, 1] = v[1].astype(BF)
        ka_copy(0).start()
        v = row_sum(3)
        ka_copy(3).wait_recv()
        sap[1, 0] = v[0].astype(BF)
        sap[1, 1] = (v[1] + rah[1].astype(F32)).astype(BF)
        ka_copy(1).start()

    def add_local():
        def body(k, _):
            i = REMOTE + k
            value = partial(i)
            j = src_ref[tab[i]]
            for n in range(OWN):
                gself[n] += only(j == n, value)
            return 0

        lax.fori_loop(0, LOCAL, body, 0)
        value = partial(N_SUB + c)
        for h in (0, 1):
            gself[h] += only(rclu_ref[0, c] == h, value)

    z_partials(HALF)
    su[HALF - 1, 0] = only(rclu_ref[0, wrap(c + HALF, NZ)] == 0, pu[HALF - 1]).astype(BF)
    ku_copy(HALF, 0).start()
    sd[HALF - 1, 1] = only(rclu_ref[0, wrap(c + HALF, NZ)] == 1, pd[HALF - 1]).astype(BF)
    kd_copy(HALF, 1).start()
    z_partials(7)
    ku_send(7, 1)
    kd_send(7, 0)
    gself[...] = dot_nt(grad_pre, ws[...]).reshape(OWN, BLK, D)
    x_send(2)
    z_partials(6)

    ku_send(7, 0)
    kd_send(7, 1)
    x_send(1)
    ku_send(6, 1)
    kd_send(6, 0)
    x_send(3)
    z_partials(5)

    ku_send(6, 0)
    kd_send(6, 1)
    b_far(2)
    ku_send(5, 1)
    kd_send(5, 0)
    x_send(0)
    z_partials(4)

    ku_send(5, 0)
    kd_send(5, 1)
    b_far(1)
    b_far(3)
    ku_send(4, 1)
    kd_send(4, 0)
    b_far(0)
    z_partials(3)

    ku_send(4, 0)
    kd_send(4, 1)
    b_near(2)
    ku_send(3, 1)
    kd_send(3, 0)
    b_near(1)
    z_partials(2)

    ku_send(3, 0)
    kd_send(3, 1)
    b_near(3)
    ku_send(2, 1)
    kd_send(2, 0)
    b_near(0)
    z_partials(1)

    ku_send(2, 0)
    kd_send(2, 1)
    a_far()
    ku_send(1, 1)
    kd_send(1, 0)
    a_near()
    ku_send(1, 0)
    kd_send(1, 1)
    add_local()

    v = row_sum(0)
    ka_copy(0).wait_recv()
    ka_copy(1).wait_recv()
    out[2] = gself[2].astype(BF)
    for h in (0, 1):
        ku_copy(1, h).wait_recv()
        kd_copy(1, h).wait_recv()
        total = gself[h] + v[h] + rap[0, h].astype(F32) + rap[1, h].astype(F32)
        total = total + ru[0, h].astype(F32) + rd[0, h].astype(F32)
        out[h] = total.astype(BF)

    for d in range(1, HALF + 1):
        for h in (0, 1):
            if has_up(d, h):
                zu_copy(d, h).wait_send()
                ku_copy(d, h).wait_send()
            if has_dn(d, h):
                zd_copy(d, h).wait_send()
                kd_copy(d, h).wait_send()
    for k in range(4):
        a_copy(k).wait_send()
        ka_copy(k).wait_send()
    for da in range(RING):
        for k in range(4):
            b_copy(da, k).wait_send()
            kb_copy(da, k).wait_send()
        for db in range(RING):
            x_copy(da, db).wait_send()
            kx_copy(da, db).wait_send()


def shards(
    features, grad_out, w_self, w_neigh, bias, tile_dst, tile_src, tile_weight, recv_sub, recv_cluster
):
    blk = (BLK, D)
    smem = pl.BlockSpec(memory_space=pltpu.SMEM)
    vmem = pl.BlockSpec(memory_space=pltpu.VMEM)
    sems = [(HALF, 2)] * 4 + [(4,)] * 2 + [(RING, 4)] * 2 + [(RING, RING)] * 2
    scratch = [
        pltpu.VMEM((TILES, BLK, BLK), BF),
        pltpu.VMEM((TILES, BLK, BLK), BF),
        pltpu.SMEM((TILES,), jnp.int32),
        pltpu.VMEM((OWN * BLK, D), F32),
        pltpu.VMEM((OWN * BLK, BLK), F32),
        pltpu.VMEM((OWN * BLK, D), F32),
        pltpu.VMEM((OWN * BLK, D), F32),
        pltpu.VMEM((OWN,) + blk, BF),
        pltpu.VMEM((OWN,) + blk, F32),
        pltpu.VMEM((HALF, 2) + blk, BF),
        pltpu.VMEM((HALF, 2) + blk, BF),
        pltpu.VMEM((RING, RING, 2) + blk, BF),
        pltpu.VMEM((RING, RING, 2) + blk, BF),
        pltpu.VMEM((HALF,) + blk, F32),
        pltpu.VMEM((HALF,) + blk, F32),
        pltpu.VMEM((HALF, 2) + blk, BF),
        pltpu.VMEM((HALF, 2) + blk, BF),
        pltpu.VMEM((HALF, 2) + blk, BF),
        pltpu.VMEM((HALF, 2) + blk, BF),
        pltpu.VMEM((RING, RING, 2) + blk, BF),
        pltpu.VMEM((RING, RING, 2) + blk, BF),
        pltpu.VMEM((RING, 2, 2) + blk, BF),
        pltpu.VMEM((RING, 2) + blk, BF),
        pltpu.VMEM((RING, 2, 2) + blk, BF),
        pltpu.VMEM((RING, 2) + blk, BF),
        pltpu.VMEM((2, 2) + blk, BF),
        pltpu.VMEM((2,) + blk, BF),
        pltpu.VMEM((2, 2) + blk, BF),
        pltpu.VMEM((2,) + blk, BF),
        pltpu.SemaphoreType.DMA,
    ] + [pltpu.SemaphoreType.DMA(shape) for shape in sems + sems]
    result = pl.pallas_call(
        kernel,
        out_shape=jax.ShapeDtypeStruct((OWN,) + blk, BF),
        in_specs=[smem] * 4 + [vmem] * 5 + [pl.BlockSpec(memory_space=pl.ANY)],
        out_specs=vmem,
        scratch_shapes=scratch,
        compiler_params=pltpu.CompilerParams(
            collective_id=0, has_side_effects=True, vmem_limit_bytes=48 * 1024 * 1024
        ),
        name="sage_layer",
    )(
        tile_src, tile_dst, recv_sub, recv_cluster,
        features.reshape((OWN,) + blk), grad_out, w_self, w_neigh, bias.reshape(1, D), tile_weight,
    )
    return result.reshape(OWN * BLK, D)


def solution(mesh):
    rows = P(("cluster", "sub"), None)
    flat = P(("cluster", "sub"))
    placed = (rows, rows, P(), P(), P(), flat, flat, P(("cluster", "sub"), None, None), rows, rows)
    return jax.shard_map(shards, mesh=mesh, in_specs=placed, out_specs=rows, check_vma=False)
```

time: 291 us -> 90.8 us (0.31)
  waiting for transfers between devices: 156 us -> 0 us
  Pallas kernels: 0 us -> 80.5 us
  starting transfers between devices: 48.2 us -> 0 us
  matrix products: 36.9 us -> 0 us
  local copies, waits for them, and re-layouts: 41.9 us -> 9.18 us
  other arithmetic: 5.04 us -> 0 us
    all_to_all x6 -> x0, waiting for transfers between devices: 156 us -> none  [the longest x1 47.1 us: shards(): lax.all_to_all(blocks[sent_cluster], 'cluster', split_axis=0, concat_axis...]
    pallas_call x0 -> x1, Pallas kernels: none -> 80.5 us  [shards(): pl.pallas_call(kernel, out_shape=jax.ShapeDtypeStruct((OWN,) + blk, BF),...]
    all_to_all x6 -> x0, starting transfers between devices: 48.2 us -> none  [the longest x1 13.4 us: shards(): lax.all_to_all(recv_cluster.reshape(cluster_count, 1), 'cluster', split_a...]
    dot_general x11 -> x0, matrix products: 36.9 us -> none  [the longest x1 10.9 us: shards(): jnp.einsum('st,tid->sid', src_onehot, returned, precision=lax.Precision.H...]
    dot_general x2 -> x0, local copies, waits for them, and re-layouts: 18.1 us -> none  [the longest x1 9.03 us: shards(): jnp.einsum('tij,tid->tjd', tile_weight, spread[tile_dst], preferred_eleme...]
    gather x4 -> x0, local copies, waits for them, and re-layouts: 11.9 us -> none  [the longest x1 4.63 us: shards(): picked = source[tile_src]]
    unnamed x24 -> x21, local copies, waits for them, and re-layouts: 1.84 us -> 9.18 us
    slice x4 -> x0, local copies, waits for them, and re-layouts: 7.29 us -> none  [the longest x2 5.42 us: shards(): partial_value[own_count:own_count + sub_count].astype(jnp.bfloat16)]
  transfers between devices with their start and end apart: 6 -> 0, of which waited for: 6 -> 0; matrix products, arithmetic and copies ran while one was open for 5% -> 0% of each run, Pallas kernels for 0% -> 0%
where the time goes in v1:
time: 90.8 us; the launch traced here: 89.7 us
  Pallas kernels  80.5 us (89%)
  local copies, waits for them, and re-layouts  9.18 us (10%)
    pallas_call x1, Pallas kernels, shards(): pl.pallas_call(kernel, out_shape=jax.ShapeDtypeStruct((OWN,) + blk, BF),...  80.5 us
    unnamed x21, local copies, waits for them, and re-layouts  9.18 us

profile of v1, /device:TPU:24, one launch (start us, length us, event | category | flops | bytes accessed | tf_op | source)
XLA Modules:
  0.0 89.7 jit_solution(7599019623514454869)
XLA Ops:
  0.0 0.0 copy-start
  0.0 1.5 %copy-done = bf16[60,128,128]{2,1,0:T(8,128)(2,1)S(1)} copy-done((bf16[60,128,128]{2,1,0:T(8,128)(2,1)S(1)}, bf16[60,128,128]{2,1,0:T(8,128)(2,1)}, u32[]{:S(2)}) %copy-start) | copy-done | bytes 1966104
  1.5 0.0 copy-start.1
  1.5 0.9 %copy-done.1 = bf16[384,256]{1,0:T(8,128)(2,1)S(1)} copy-done((bf16[384,256]{1,0:T(8,128)(2,1)S(1)}, bf16[384,256]{1,0:T(8,128)(2,1)}, u32[]{:S(2)}) %copy-start.1) | copy-done | bytes 196632
  2.5 0.0 copy-start.2
  2.5 0.9 %copy-done.2 = bf16[384,256]{1,0:T(8,128)(2,1)S(1)} copy-done((bf16[384,256]{1,0:T(8,128)(2,1)S(1)}, bf16[384,256]{1,0:T(8,128)(2,1)}, u32[]{:S(2)}) %copy-start.2) | copy-done | bytes 196632
  3.4 0.0 copy-start.3
  3.4 0.9 %copy-done.3 = bf16[256,256]{1,0:T(8,128)(2,1)S(1)} copy-done((bf16[256,256]{1,0:T(8,128)(2,1)S(1)}, bf16[256,256]{1,0:T(8,128)(2,1)}, u32[]{:S(2)}) %copy-start.3) | copy-done | bytes 131096
  4.3 0.0 copy-start.4
  4.3 0.9 %copy-done.4 = bf16[256,256]{1,0:T(8,128)(2,1)S(1)} copy-done((bf16[256,256]{1,0:T(8,128)(2,1)S(1)}, bf16[256,256]{1,0:T(8,128)(2,1)}, u32[]{:S(2)}) %copy-start.4) | copy-done | bytes 131096
  5.2 0.0 copy-start.5
  5.2 0.7 copy-done.5
  5.9 0.0 copy-start.6
  5.9 0.7 copy-done.6
  6.5 0.0 copy-start.7
  6.5 0.7 copy-done.7
  7.2 0.0 copy-start.8
  7.2 0.7 copy-done.8
  7.9 0.0 copy-start.9
  7.9 0.7 copy-done.9
  8.5 80.5 %sage_layer.1 = bf16[3,128,256]{2,1,0:T(8,128)(2,1)S(1)} custom-call(s32[60]{0:T(128)S(1)} %copy-done.6, s32[60]{0:T(128)S(1)} %copy-done.7, s32[1,32]{1,0:T(1,128)S(1)} %copy-done.8, s32[1,16]{1,0:T(1,128)S(1)} %copy-done.9, bf16[3,128,256]{2,1,0:T(8,128)(2,1)S(1)} %bitcast.4, bf16[384,256]{1,0:T(8,128)(2,1)S(1)} %copy-done.2, ...), custom_call_target="tpu_custom_call" | custom-call | tf_op jit(solution)/shard_map/sage_layer/pallas_call | solution.py:595
  89.0 0.7 copy.12
Async XLA Ops:
  0.0 1.5 %copy-start = (bf16[60,128,128]{2,1,0:T(8,128)(2,1)S(1)}, bf16[60,128,128]{2,1,0:T(8,128)(2,1)}, u32[]{:S(2)}) copy-start(bf16[60,128,128]{2,1,0:T(8,128)(2,1)} %tiles_hbm.1) | copy-start | bytes 5898244
  1.5 0.9 %copy-start.1 = (bf16[384,256]{1,0:T(8,128)(2,1)S(1)}, bf16[384,256]{1,0:T(8,128)(2,1)}, u32[]{:S(2)}) copy-start(bf16[384,256]{1,0:T(8,128)(2,1)} %param.10) | copy-start | bytes 589828
  2.5 0.9 %copy-start.2 = (bf16[384,256]{1,0:T(8,128)(2,1)S(1)}, bf16[384,256]{1,0:T(8,128)(2,1)}, u32[]{:S(2)}) copy-start(bf16[384,256]{1,0:T(8,128)(2,1)} %gout.1) | copy-start | bytes 589828
  3.4 0.9 %copy-start.3 = (bf16[256,256]{1,0:T(8,128)(2,1)S(1)}, bf16[256,256]{1,0:T(8,128)(2,1)}, u32[]{:S(2)}) copy-start(bf16[256,256]{1,0:T(8,128)(2,1)} %ws.1) | copy-start | bytes 393220
  4.3 0.9 %copy-start.4 = (bf16[256,256]{1,0:T(8,128)(2,1)S(1)}, bf16[256,256]{1,0:T(8,128)(2,1)}, u32[]{:S(2)}) copy-start(bf16[256,256]{1,0:T(8,128)(2,1)} %wn.1) | copy-start | bytes 393220
  5.2 0.7 copy-start.5
  5.9 0.7 copy-start.6
  6.5 0.7 copy-start.7
  7.2 0.7 copy-start.8
  7.9 0.7 copy-start.9

commit v2 on v1

v2 whole, which is shorter than its diff:
```python
import functools

import jax
import jax.numpy as jnp
from jax import lax
from jax.experimental import pallas as pl
from jax.experimental.pallas import tpu as pltpu
from jax.sharding import PartitionSpec as P

MESH = pl.DeviceIdType.MESH
BF = jnp.bfloat16
F32 = jnp.float32
NZ = 16
RING = 4
HALF = NZ // 2
BLK = 128
D = 256
OWN = 3
TILES = 60
N_SUB = 32
REMOTE = N_SUB + NZ
LOCAL = TILES - REMOTE
SLOTS = 128
SKIP_F = 0
SKIP_B = 0
CHUNKS = 4
PER = CHUNKS // 2
ROWS = BLK // PER
VMEM_BYTES = 62 * 1024 * 1024


def wrap(value, size):
    return lax.rem(value + size, size)


def dot_nt(left, right):
    return lax.dot_general(left, right, (((1,), (1,)), ((), ())), preferred_element_type=F32)


def kernel(
    src_hbm, dst_hbm, rsub_hbm, rclu_hbm,
    feat_hbm, gout_hbm, ws_hbm, wn_hbm, bias_hbm, tiles_hbm,
    out,
    src_ref, dst_ref, rsub_ref, rclu_ref, feat, gout, ws, wn, bias,
    src_row, tab_row, w, wt, tab, acc, deg, pre, inv, spread, gself,
    zu, zd, gs, gb,
    pu, pd, su, sd, ru, rd,
    sb, rb, sbp, sbh, rbp, rbh, sap, sah, rap, rah,
    in_s,
    zu_s, zu_r, zd_s, zd_r, a_s, a_r, b_s, b_r, x_s, x_r,
    ku_s, ku_r, kd_s, kd_r, ka_s, ka_r, kb_s, kb_r, kx_s, kx_r,
):
    c = lax.axis_index("cluster")
    s = lax.axis_index("sub")
    core = lax.rem(s, 2)
    x = lax.rem(s // 2, RING)
    y = s // (2 * RING)
    a = x * (1 - core) + y * core
    b = y * (1 - core) + x * core

    def at(da, db, which):
        aa = wrap(a + da, RING)
        bb = wrap(b + db, RING)
        xx = aa * (1 - core) + bb * core
        yy = bb * (1 - core) + aa * core
        return (yy * RING + xx) * 2 + which

    up = (wrap(c + 1, NZ), s)
    dn = (wrap(c - 1, NZ), s)
    up2 = (wrap(c + 2, NZ), s)
    dn2 = (wrap(c - 2, NZ), s)
    ap = (c, at(1, 0, core))
    am = (c, at(-1, 0, core))
    bp = (c, at(0, 1, core))
    bm = (c, at(0, -1, core))
    sib = (c, at(0, 0, 1 - core))

    def copy(source, target, send, recv, device):
        return pltpu.make_async_remote_copy(
            src_ref=source, dst_ref=target, send_sem=send, recv_sem=recv,
            device_id=device, device_id_type=MESH,
        )

    def same_index(da, db):
        return at(-da, -db, core)

    def other_index(da, db):
        return at(-db, -da, 1 - core)

    inputs = (
        (feat_hbm, feat), (src_hbm, src_ref), (src_hbm, src_row), (dst_hbm, dst_ref), (rsub_hbm, rsub_ref),
        (rclu_hbm, rclu_ref), (ws_hbm, ws), (bias_hbm, bias), (tiles_hbm, w), (wn_hbm, wn),
        (gout_hbm, gout),
    )
    loads = [pltpu.make_async_copy(*pair, in_s.at[k]) for k, pair in enumerate(inputs)]
    for load in loads:
        load.start()
    barrier = pltpu.get_barrier_semaphore()
    for device in (up, dn, up2, dn2, ap, am, bp, bm, sib):
        pl.semaphore_signal(barrier, inc=1, device_id=device, device_id_type=MESH)
    pl.semaphore_wait(barrier, 9)

    def rows_of(q):
        return q // PER, pl.ds(q % PER * ROWS, ROWS)

    def is_far(up_way, q):
        return (q < PER) == up_way

    def has(up_way, d, q):
        return d < HALF or (d == HALF and is_far(up_way, q))

    def z_copy(up_way, d, q):
        buf, send, recv = (zu, zu_s, zu_r) if up_way else (zd, zd_s, zd_r)
        h, rows = rows_of(q)
        source = buf.at[d - 2, h, rows] if d > 1 else feat_hbm.at[h, rows]
        device = up if up_way else dn
        if SKIP_F and d == 2 and is_far(up_way, q):
            source = feat_hbm.at[h, rows]
            device = up2 if up_way else dn2
        return copy(source, buf.at[d - 1, h, rows], send.at[d - 1, q], recv.at[d - 1, q], device)

    def z_start():
        for d, far in ((1, False), (2, True), (1, True)) if SKIP_F else ((1, True), (1, False)):
            for q in range(CHUNKS):
                for up_way in (True, False):
                    if is_far(up_way, q) == far:
                        z_copy(up_way, d, q).start()

    def z_step(r, far):
        d = r + 1 if far else r
        if SKIP_F and d == 1 and far:
            return
        for q in range(PER):
            for up_way in (True, False):
                p = q if far == up_way else q + PER
                z_copy(up_way, d, p).wait_recv()
                if has(up_way, d + 1, p):
                    z_copy(up_way, d + 1, p).start()

    def z_first():
        if not SKIP_F:
            return
        for q in range(CHUNKS):
            for up_way in (True, False):
                if is_far(up_way, q):
                    z_copy(up_way, 1, q).wait_recv()

    own = feat_hbm.at[pl.ds(0, 2)]

    def a_copy(k):
        source, target, device = (
            (own, gs.at[1, 0], ap),
            (own, gs.at[3, 0], am),
            (gs.at[1, 0, 0], gs.at[2, 0, 0], ap),
            (gs.at[3, 0, 1], gs.at[2, 0, 1], am),
        )[k]
        return copy(source, target, a_s.at[k], a_r.at[k], device)

    def b_copy(da, k):
        source, target, device = (
            (gs.at[da, 0] if da else own, gs.at[da, 1], bp),
            (gs.at[da, 0] if da else own, gs.at[da, 3], bm),
            (gs.at[da, 1, 0], gs.at[da, 2, 0], bp),
            (gs.at[da, 3, 1], gs.at[da, 2, 1], bm),
        )[k]
        return copy(source, target, b_s.at[da, k], b_r.at[da, k], device)

    def x_copy(da, db):
        source = gs.at[da, db]
        if da == 0 and isinstance(db, int) and db == 0:
            source = own
        return copy(source, gb.at[da, db], x_s.at[da, db], x_r.at[da, db], sib)

    def a_start():
        a_copy(0).start()
        a_copy(1).start()

    def a_mid():
        a_copy(0).wait_recv()
        a_copy(2).start()
        a_copy(1).wait_recv()
        a_copy(3).start()
        for da in (1, 3):
            b_start(da)
            x_copy(da, 0).start()

    def a_end():
        a_copy(2).wait_recv()
        a_copy(3).wait_recv()
        b_start(2)
        x_copy(2, 0).start()

    def b_start(da):
        b_copy(da, 0).start()
        b_copy(da, 1).start()

    def b_mid(da):
        b_copy(da, 0).wait_recv()
        b_copy(da, 2).start()
        b_copy(da, 1).wait_recv()
        b_copy(da, 3).start()
        x_copy(da, 1).start()
        x_copy(da, 3).start()

    def b_end(da):
        b_copy(da, 2).wait_recv()
        b_copy(da, 3).wait_recv()
        x_copy(da, 2).start()

    def find_tiles():
        row = lax.broadcasted_iota(jnp.int32, (TILES, TILES), 0)
        col = lax.broadcasted_iota(jnp.int32, (TILES, TILES), 1)
        by_col = jnp.broadcast_to(src_row[...], (TILES, TILES))
        earlier = jnp.where(jnp.logical_and(by_col < OWN, col < row), 1, 0)
        earlier = jnp.sum(earlier, axis=1, keepdims=True)
        src = jnp.broadcast_to(src_row[...], (SLOTS, TILES)).T
        place = jnp.where(src < OWN, REMOTE + earlier, src - OWN)
        tile = lax.broadcasted_iota(jnp.int32, (TILES, SLOTS), 0)
        slot = lax.broadcasted_iota(jnp.int32, (TILES, SLOTS), 1)
        tab_row[...] = jnp.sum(jnp.where(place == slot, tile, 0), axis=0, keepdims=True)
        move = pltpu.make_async_copy(tab_row, tab, in_s.at[0])
        move.start()
        return move

    def transpose_tiles(first, count):
        def body(t, _):
            wt[t] = w[t].T
            return 0

        lax.fori_loop(first, first + count, body, 0)

    def tile_row(entries):
        tiles = [tab[0, i] for i in entries]
        zero = jnp.zeros((BLK, BLK), BF)
        return jnp.concatenate(
            [
                jnp.concatenate([jnp.where(dst_ref[0, t] == k, w[t], zero) for t in tiles], axis=1)
                for k in range(OWN)
            ],
            axis=0,
        )

    def accumulate(entries, blocks, count=True):
        left = tile_row(entries)
        acc[...] += jnp.dot(left, jnp.concatenate(blocks, axis=0), preferred_element_type=F32)
        if count:
            add_degree(left)

    def add_degree(left):
        ones = jnp.ones((left.shape[1], BLK), BF)
        deg[...] += jnp.dot(left, ones, preferred_element_type=F32)

    def invert_degree():
        late = [wrap(c - 7, NZ), wrap(c + 7, NZ), wrap(c + HALF, NZ), c]
        add_degree(tile_row([N_SUB + r for r in late]))
        scale = 1.0 / (deg[...] + 1.0)
        inv[...] = jnp.concatenate([scale, scale], axis=1)

    def z_pair(d):
        r0, r1 = wrap(c - d, NZ), wrap(c + d, NZ)
        block0 = jnp.where(rclu_ref[0, r0] == 0, zu[d - 1, 0], zu[d - 1, 1])
        block1 = jnp.where(rclu_ref[0, r1] == 0, zd[d - 1, 0], zd[d - 1, 1])
        accumulate([N_SUB + r0, N_SUB + r1], [block0, block1], d < 7)

    def z_last():
        r0 = wrap(c + HALF, NZ)
        block0 = jnp.where(rclu_ref[0, r0] == 0, zu[HALF - 1, 0], zd[HALF - 1, 1])
        block1 = jnp.where(rclu_ref[0, c] == 0, feat[0], feat[1])
        accumulate([N_SUB + r0, N_SUB + c], [block0, block1], False)

    def sub_pairs(da, first):
        entries, blocks = [], []
        for db in (first, first + 1):
            x_copy(da, db).wait_recv()
            for p, buf in ((same_index(da, db), gs), (other_index(da, db), gb)):
                entries.append(p)
                blocks.append(jnp.where(rsub_ref[0, p] == 0, buf[da, db, 0], buf[da, db, 1]))
        accumulate(entries, blocks)

    def local_tiles(first):
        entries = [REMOTE + first + k for k in range(4)]
        accumulate(entries, [feat[src_ref[0, tab[0, i]]] for i in entries])

    def self_product():
        rows = feat[...].reshape(OWN * BLK, D)
        pre[...] = jnp.dot(rows, ws[...], preferred_element_type=F32) + bias[...]

    z_start()
    a_start()
    b_start(0)
    x_copy(0, 0).start()
    acc[...] = jnp.zeros_like(acc)
    deg[...] = jnp.zeros_like(deg)
    for load in loads:
        load.wait()
    gs[0, 0] = feat[0:2]
    found = find_tiles()
    self_product()
    transpose_tiles(0, 12)
    found.wait()

    z_step(0, True)
    transpose_tiles(12, 12)
    z_step(1, False)
    transpose_tiles(24, 8)
    z_step(1, True)
    a_mid()
    b_mid(0)
    z_pair(1)
    z_step(2, False)
    z_first()
    local_tiles(0)
    z_step(2, True)
    a_end()
    z_pair(2)
    z_step(3, False)
    transpose_tiles(32, 8)
    z_step(3, True)
    b_mid(1)
    b_mid(3)
    b_end(0)
    z_pair(3)
    z_step(4, False)
    transpose_tiles(40, 8)
    sub_pairs(0, 0)
    z_step(4, True)
    b_mid(2)
    b_end(1)
    b_end(3)
    z_pair(4)
    z_step(5, False)
    transpose_tiles(48, 6)
    sub_pairs(0, 2)
    z_step(5, True)
    b_end(2)
    z_pair(5)
    sub_pairs(1, 0)
    z_step(6, False)
    sub_pairs(1, 2)
    transpose_tiles(54, 6)
    local_tiles(4)
    z_step(6, True)
    z_pair(6)
    sub_pairs(3, 0)
    sub_pairs(3, 2)
    z_step(7, False)
    sub_pairs(2, 0)
    sub_pairs(2, 2)
    local_tiles(8)
    invert_degree()
    z_pair(7)
    z_step(7, True)
    z_last()

    mean = (acc[...] * inv[...]).astype(BF)
    v = pre[...] + jnp.dot(mean, wn[...], preferred_element_type=F32)
    k0, k1 = 0.7978845608028654, 0.044715
    square = v * v
    th = jnp.tanh(k0 * v * (1.0 + k1 * square))
    slope = 0.5 * (1.0 + th) + 0.5 * v * (1.0 - th * th) * (k0 * (1.0 + 3.0 * k1 * square))
    grad_pre = (gout[...].astype(F32) * slope).astype(BF)
    spread[...] = (dot_nt(grad_pre, wn[...]) * inv[...]).astype(BF).reshape(OWN, BLK, D)

    def partial(i):
        t = tab[0, i]
        return jnp.dot(wt[t], spread[dst_ref[0, t]], preferred_element_type=F32)

    def only(keep, value):
        return jnp.where(keep, value, jnp.zeros_like(value))

    def k_copy(up_way, d, q):
        out_buf, in_buf, send, recv = (su, ru, ku_s, ku_r) if up_way else (sd, rd, kd_s, kd_r)
        h, rows = rows_of(q)
        slot, device = d - 1, up if up_way else dn
        if SKIP_B and is_far(up_way, q) and d == 2:
            slot, device = 0, up2 if up_way else dn2
        if SKIP_B and is_far(up_way, q) and d == 1:
            slot = 1
        return copy(
            out_buf.at[d - 1, h, rows], in_buf.at[slot, h, rows], send.at[slot, q], recv.at[slot, q], device
        )

    def k_send(up_way, d, q):
        out_buf, in_buf, part = (su, ru, pu) if up_way else (sd, rd, pd)
        h, rows = rows_of(q)
        far = is_far(up_way, q)
        owner = wrap(c + d if up_way else c - d, NZ)
        value = only(rclu_ref[0, owner] == h, part[d - 1, rows])
        if (SKIP_B < d < HALF) if far else d < HALF - 1:
            k_copy(up_way, d + 1, q).wait_recv()
            value = value + in_buf[d, h, rows].astype(F32)
        out_buf[d - 1, h, rows] = value.astype(BF)
        k_copy(up_way, d, q).start()

    def k_step(d, far):
        for q in range(PER):
            for up_way in (True, False):
                k_send(up_way, d, q if far == up_way else q + PER)

    def z_partials(d):
        pu[d - 1] = partial(N_SUB + wrap(c + d, NZ))
        pd[d - 1] = partial(N_SUB + wrap(c - d, NZ))

    def kx_copy(da, db):
        return copy(sb.at[da, db], rb.at[da, db], kx_s.at[da, db], kx_r.at[da, db], sib)

    def x_send(da):
        def body(db, _):
            p = other_index(da, db)
            value = partial(p)
            for h in (0, 1):
                sb[da, db, h] = only(rsub_ref[0, p] == h, value).astype(BF)
            kx_copy(da, db).start()
            return 0

        lax.fori_loop(0, RING, body, 0)

    def kb_copy(da, k):
        source, target, device = (
            (sbp.at[da, 0], rbp.at[da, 0], bm),
            (sbp.at[da, 1], rbp.at[da, 1], bp),
            (sbh.at[da, 0], rbh.at[da, 0], bm),
            (sbh.at[da, 1], rbh.at[da, 1], bp),
        )[k]
        return copy(source, target, kb_s.at[da, k], kb_r.at[da, k], device)

    def ka_copy(k):
        source, target, device = (
            (sap.at[0], rap.at[0], am),
            (sap.at[1], rap.at[1], ap),
            (sah.at[0], rah.at[0], am),
            (sah.at[1], rah.at[1], ap),
        )[k]
        return copy(source, target, ka_s.at[k], ka_r.at[k], device)

    def chip_sum(da, db):
        p = same_index(da, db)
        value = partial(p)
        kx_copy(da, db).wait_recv()
        return [
            only(rsub_ref[0, p] == h, value) + rb[da, db, h].astype(F32) for h in (0, 1)
        ]

    def b_far(da):
        v0, v1 = chip_sum(da, 2)
        sbh[da, 0] = v0.astype(BF)
        kb_copy(da, 2).start()
        sbh[da, 1] = v1.astype(BF)
        kb_copy(da, 3).start()

    def b_near(da):
        v0, v1 = chip_sum(da, 1)
        sbp[da, 0, 1] = v1.astype(BF)
        kb_copy(da, 2).wait_recv()
        sbp[da, 0, 0] = (v0 + rbh[da, 0].astype(F32)).astype(BF)
        kb_copy(da, 0).start()
        v0, v1 = chip_sum(da, 3)
        sbp[da, 1, 0] = v0.astype(BF)
        kb_copy(da, 3).wait_recv()
        sbp[da, 1, 1] = (v1 + rbh[da, 1].astype(F32)).astype(BF)
        kb_copy(da, 1).start()

    def row_sum(da):
        v = chip_sum(da, 0)
        kb_copy(da, 0).wait_recv()
        kb_copy(da, 1).wait_recv()
        return [v[h] + rbp[da, 0, h].astype(F32) + rbp[da, 1, h].astype(F32) for h in (0, 1)]

    def a_far():
        v = row_sum(2)
        sah[0] = v[0].astype(BF)
        ka_copy(2).start()
        sah[1] = v[1].astype(BF)
        ka_copy(3).start()

    def a_near():
        v = row_sum(1)
        ka_copy(2).wait_recv()
        sap[0, 0] = (v[0] + rah[0].astype(F32)).astype(BF)
        sap[0, 1] = v[1].astype(BF)
        ka_copy(0).start()
        v = row_sum(3)
        ka_copy(3).wait_recv()
        sap[1, 0] = v[0].astype(BF)
        sap[1, 1] = (v[1] + rah[1].astype(F32)).astype(BF)
        ka_copy(1).start()

    def add_local():
        def body(k, _):
            i = REMOTE + k
            value = partial(i)
            j = src_ref[0, tab[0, i]]
            for n in range(OWN):
                gself[n] += only(j == n, value)
            return 0

        lax.fori_loop(0, LOCAL, body, 0)
        value = partial(N_SUB + c)
        for h in (0, 1):
            gself[h] += only(rclu_ref[0, c] == h, value)

    z_partials(HALF)
    k_step(HALF, True)
    z_partials(7)
    k_step(7, False)
    z_partials(1)
    if SKIP_B:
        k_step(1, True)
    x_send(2)
    z_partials(6)

    k_step(7, True)
    x_send(1)
    k_step(6, False)
    x_send(3)
    z_partials(5)

    k_step(6, True)
    b_far(2)
    k_step(5, False)
    x_send(0)
    z_partials(4)

    k_step(5, True)
    b_far(1)
    b_far(3)
    k_step(4, False)
    b_far(0)
    z_partials(3)

    k_step(4, True)
    b_near(2)
    k_step(3, False)
    b_near(1)
    z_partials(2)

    k_step(3, True)
    b_near(3)
    k_step(2, False)
    b_near(0)

    k_step(2, True)
    a_far()
    k_step(1, False)
    a_near()
    if not SKIP_B:
        k_step(1, True)
    gself[...] = dot_nt(grad_pre, ws[...]).reshape(OWN, BLK, D)
    add_local()

    v = row_sum(0)
    ka_copy(0).wait_recv()
    ka_copy(1).wait_recv()
    out[2] = gself[2].astype(BF)
    for q in range(CHUNKS):
        h, rows = rows_of(q)
        total = gself[h, rows] + v[h][q % PER * ROWS : (q % PER + 1) * ROWS]
        total = total + rap[0, h, rows].astype(F32) + rap[1, h, rows].astype(F32)
        for up_way, buf in ((True, ru), (False, rd)):
            far = SKIP_B and is_far(up_way, q)
            if far:
                k_copy(up_way, 1, q).wait_recv()
                total = total + buf[1, h, rows].astype(F32)
            k_copy(up_way, 2 if far else 1, q).wait_recv()
            total = total + buf[0, h, rows].astype(F32)
        out[h, rows] = total.astype(BF)

    for d in range(1, HALF + 1):
        for q in range(CHUNKS):
            for up_way in (True, False):
                if has(up_way, d, q):
                    z_copy(up_way, d, q).wait_send()
                    k_copy(up_way, d, q).wait_send()
    for k in range(4):
        a_copy(k).wait_send()
        ka_copy(k).wait_send()
    for da in range(RING):
        for k in range(4):
            b_copy(da, k).wait_send()
            kb_copy(da, k).wait_send()
        for db in range(RING):
            x_copy(da, db).wait_send()
            kx_copy(da, db).wait_send()


def shards(
    features, grad_out, w_self, w_neigh, bias, tile_dst, tile_src, tile_weight, recv_sub, recv_cluster
):
    blk = (BLK, D)
    vmem = pl.BlockSpec(memory_space=pltpu.VMEM)
    sems = [(HALF, CHUNKS)] * 4 + [(4,)] * 2 + [(RING, 4)] * 2 + [(RING, RING)] * 2
    scratch = [
        pltpu.SMEM((1, TILES), jnp.int32),
        pltpu.SMEM((1, TILES), jnp.int32),
        pltpu.SMEM((1, N_SUB), jnp.int32),
        pltpu.SMEM((1, NZ), jnp.int32),
        pltpu.VMEM((OWN,) + blk, BF),
        pltpu.VMEM((OWN * BLK, D), BF),
        pltpu.VMEM((D, D), BF),
        pltpu.VMEM((D, D), BF),
        pltpu.VMEM((1, D), F32),
        pltpu.VMEM((1, TILES), jnp.int32),
        pltpu.VMEM((1, SLOTS), jnp.int32),
        pltpu.VMEM((TILES, BLK, BLK), BF),
        pltpu.VMEM((TILES, BLK, BLK), BF),
        pltpu.SMEM((1, SLOTS), jnp.int32),
        pltpu.VMEM((OWN * BLK, D), F32),
        pltpu.VMEM((OWN * BLK, BLK), F32),
        pltpu.VMEM((OWN * BLK, D), F32),
        pltpu.VMEM((OWN * BLK, D), F32),
        pltpu.VMEM((OWN,) + blk, BF),
        pltpu.VMEM((OWN,) + blk, F32),
        pltpu.VMEM((HALF, 2) + blk, BF),
        pltpu.VMEM((HALF, 2) + blk, BF),
        pltpu.VMEM((RING, RING, 2) + blk, BF),
        pltpu.VMEM((RING, RING, 2) + blk, BF),
        pltpu.VMEM((HALF,) + blk, F32),
        pltpu.VMEM((HALF,) + blk, F32),
        pltpu.VMEM((HALF, 2) + blk, BF),
        pltpu.VMEM((HALF, 2) + blk, BF),
        pltpu.VMEM((HALF, 2) + blk, BF),
        pltpu.VMEM((HALF, 2) + blk, BF),
        pltpu.VMEM((RING, RING, 2) + blk, BF),
        pltpu.VMEM((RING, RING, 2) + blk, BF),
        pltpu.VMEM((RING, 2, 2) + blk, BF),
        pltpu.VMEM((RING, 2) + blk, BF),
        pltpu.VMEM((RING, 2, 2) + blk, BF),
        pltpu.VMEM((RING, 2) + blk, BF),
        pltpu.VMEM((2, 2) + blk, BF),
        pltpu.VMEM((2,) + blk, BF),
        pltpu.VMEM((2, 2) + blk, BF),
        pltpu.VMEM((2,) + blk, BF),
        pltpu.SemaphoreType.DMA((11,)),
    ] + [pltpu.SemaphoreType.DMA(shape) for shape in sems + sems]
    result = pl.pallas_call(
        kernel,
        out_shape=jax.ShapeDtypeStruct((OWN,) + blk, BF),
        in_specs=[pl.BlockSpec(memory_space=pl.ANY)] * 10,
        out_specs=vmem,
        scratch_shapes=scratch,
        compiler_params=pltpu.CompilerParams(
            collective_id=0, has_side_effects=True, vmem_limit_bytes=VMEM_BYTES
        ),
        name="sage_layer",
    )(
        tile_src.reshape(1, TILES), tile_dst.reshape(1, TILES), recv_sub, recv_cluster,
        features.reshape((OWN,) + blk), grad_out, w_self, w_neigh, bias.reshape(1, D), tile_weight,
    )
    return result.reshape(OWN * BLK, D)


def solution(mesh):
    rows = P(("cluster", "sub"), None)
    flat = P(("cluster", "sub"))
    placed = (rows, rows, P(), P(), P(), flat, flat, P(("cluster", "sub"), None, None), rows, rows)
    return jax.shard_map(shards, mesh=mesh, in_specs=placed, out_specs=rows, check_vma=False)
```

time: 90.8 us -> 79 us (0.87)
  local copies, waits for them, and re-layouts: 9.18 us -> 1.62 us
  Pallas kernels: 80.5 us -> 77 us
    unnamed x21 -> x1, local copies, waits for them, and re-layouts: 9.18 us -> 1.62 us
    pallas_call x1, Pallas kernels: 80.5 us -> 77 us  [shards(): pl.pallas_call(kernel, out_shape=jax.ShapeDtypeStruct((OWN,) + blk, BF),...]
where the time goes in v2:
time: 79 us; the launch traced here: 78.6 us
  Pallas kernels  77 us (97%)
  local copies, waits for them, and re-layouts  1.62 us (2%)
    pallas_call x1, Pallas kernels, shards(): pl.pallas_call(kernel, out_shape=jax.ShapeDtypeStruct((OWN,) + blk, BF),...  77 us
    unnamed x1, local copies, waits for them, and re-layouts  1.62 us

profile of v2, /device:TPU:24, one launch (start us, length us, event | category | flops | bytes accessed | tf_op | source)
XLA Modules:
  0.0 78.6 jit_solution(7094971576709442662)
XLA Ops:
  0.0 77.0 %sage_layer.1 = bf16[3,128,256]{2,1,0:T(8,128)(2,1)} custom-call(s32[1,60]{1,0:T(1,128)} %bitcast.8, s32[1,60]{1,0:T(1,128)} %bitcast.9, s32[1,32]{1,0:T(1,128)} %rsub_hbm.1, s32[1,16]{1,0:T(1,128)} %rclu_hbm.1, bf16[3,128,256]{2,1,0:T(8,128)(2,1)} %bitcast.6, bf16[384,256]{1,0:T(8,128)(2,1)} %gout_hbm.1, bf16[256,256]{1,0:T(8,128)(2,1)} %ws_hbm.1, ...), custom_call_target="tpu_custom_call" | custom-call | tf_op jit(solution)/shard_map/sage_layer/pallas_call | solution.py:635
  77.0 1.6 %copy.12 = bf16[384,256]{1,0:T(8,128)(2,1)} copy(bf16[384,256]{1,0:T(8,128)(2,1)} %bitcast.5) | data formatting | bytes 393216

commit v3 on v2

--- a/solution.py
+++ b/solution.py
@@ -21,8 +21,6 @@
 REMOTE = N_SUB + NZ
 LOCAL = TILES - REMOTE
 SLOTS = 128
-SKIP_F = 0
-SKIP_B = 0
 CHUNKS = 4
 PER = CHUNKS // 2
 ROWS = BLK // PER
@@ -40,8 +38,8 @@
 def kernel(
     src_hbm, dst_hbm, rsub_hbm, rclu_hbm,
     feat_hbm, gout_hbm, ws_hbm, wn_hbm, bias_hbm, tiles_hbm,
-    out,
-    src_ref, dst_ref, rsub_ref, rclu_ref, feat, gout, ws, wn, bias,
+    out_hbm,
+    out, src_ref, dst_ref, rsub_ref, rclu_ref, feat, gout, ws, wn, bias,
     src_row, tab_row, w, wt, tab, acc, deg, pre, inv, spread, gself,
     zu, zd, gs, gb,
     pu, pd, su, sd, ru, rd,
@@ -67,8 +65,6 @@
 
     up = (wrap(c + 1, NZ), s)
     dn = (wrap(c - 1, NZ), s)
-    up2 = (wrap(c + 2, NZ), s)
-    dn2 = (wrap(c - 2, NZ), s)
     ap = (c, at(1, 0, core))
     am = (c, at(-1, 0, core))
     bp = (c, at(0, 1, core))
@@ -81,24 +77,35 @@
             device_id=device, device_id_type=MESH,
         )
 
+    sent = []
+
+    def start(make, *args):
+        make(*args).start()
+        sent.append((make, args))
+
+    def drain(keep):
+        while len(sent) > keep:
+            make, args = sent.pop(0)
+            make(*args).wait_send()
+
     def same_index(da, db):
         return at(-da, -db, core)
 
     def other_index(da, db):
         return at(-db, -da, 1 - core)
 
+    barrier = pltpu.get_barrier_semaphore()
+    for device in (up, dn, ap, am, bp, bm, sib):
+        pl.semaphore_signal(barrier, inc=1, device_id=device, device_id_type=MESH)
     inputs = (
-        (feat_hbm, feat), (src_hbm, src_ref), (src_hbm, src_row), (dst_hbm, dst_ref), (rsub_hbm, rsub_ref),
-        (rclu_hbm, rclu_ref), (ws_hbm, ws), (bias_hbm, bias), (tiles_hbm, w), (wn_hbm, wn),
+        (src_hbm, src_row), (feat_hbm, feat), (ws_hbm, ws), (bias_hbm, bias), (src_hbm, src_ref),
+        (dst_hbm, dst_ref), (rsub_hbm, rsub_ref), (rclu_hbm, rclu_ref), (tiles_hbm, w), (wn_hbm, wn),
         (gout_hbm, gout),
     )
     loads = [pltpu.make_async_copy(*pair, in_s.at[k]) for k, pair in enumerate(inputs)]
     for load in loads:
         load.start()
-    barrier = pltpu.get_barrier_semaphore()
-    for device in (up, dn, up2, dn2, ap, am, bp, bm, sib):
-        pl.semaphore_signal(barrier, inc=1, device_id=device, device_id_type=MESH)
-    pl.semaphore_wait(barrier, 9)
+    pl.semaphore_wait(barrier, 7)
 
     def rows_of(q):
         return q // PER, pl.ds(q % PER * ROWS, ROWS)
@@ -114,36 +121,22 @@
         h, rows = rows_of(q)
         source = buf.at[d - 2, h, rows] if d > 1 else feat_hbm.at[h, rows]
         device = up if up_way else dn
-        if SKIP_F and d == 2 and is_far(up_way, q):
-            source = feat_hbm.at[h, rows]
-            device = up2 if up_way else dn2
         return copy(source, buf.at[d - 1, h, rows], send.at[d - 1, q], recv.at[d - 1, q], device)
 
     def z_start():
-        for d, far in ((1, False), (2, True), (1, True)) if SKIP_F else ((1, True), (1, False)):
-            for q in range(CHUNKS):
+        for far in (True, False):
+            for q in range(PER):
                 for up_way in (True, False):
-                    if is_far(up_way, q) == far:
-                        z_copy(up_way, d, q).start()
+                    start(z_copy, up_way, 1, q if far == up_way else q + PER)
 
     def z_step(r, far):
         d = r + 1 if far else r
-        if SKIP_F and d == 1 and far:
-            return
         for q in range(PER):
             for up_way in (True, False):
                 p = q if far == up_way else q + PER
                 z_copy(up_way, d, p).wait_recv()
                 if has(up_way, d + 1, p):
-                    z_copy(up_way, d + 1, p).start()
-
-    def z_first():
-        if not SKIP_F:
-            return
-        for q in range(CHUNKS):
-            for up_way in (True, False):
-                if is_far(up_way, q):
-                    z_copy(up_way, 1, q).wait_recv()
+                    start(z_copy, up_way, d + 1, p)
 
     own = feat_hbm.at[pl.ds(0, 2)]
 
@@ -172,40 +165,40 @@
         return copy(source, gb.at[da, db], x_s.at[da, db], x_r.at[da, db], sib)
 
     def a_start():
-        a_copy(0).start()
-        a_copy(1).start()
+        start(a_copy, 0)
+        start(a_copy, 1)
 
     def a_mid():
         a_copy(0).wait_recv()
-        a_copy(2).start()
+        start(a_copy, 2)
         a_copy(1).wait_recv()
-        a_copy(3).start()
+        start(a_copy, 3)
         for da in (1, 3):
             b_start(da)
-            x_copy(da, 0).start()
+            start(x_copy, da, 0)
 
     def a_end():
         a_copy(2).wait_recv()
         a_copy(3).wait_recv()
         b_start(2)
-        x_copy(2, 0).start()
+        start(x_copy, 2, 0)
 
     def b_start(da):
-        b_copy(da, 0).start()
-        b_copy(da, 1).start()
+        start(b_copy, da, 0)
+        start(b_copy, da, 1)
 
     def b_mid(da):
         b_copy(da, 0).wait_recv()
-        b_copy(da, 2).start()
+        start(b_copy, da, 2)
         b_copy(da, 1).wait_recv()
-        b_copy(da, 3).start()
-        x_copy(da, 1).start()
-        x_copy(da, 3).start()
+        start(b_copy, da, 3)
+        start(x_copy, da, 1)
+        start(x_copy, da, 3)
 
     def b_end(da):
         b_copy(da, 2).wait_recv()
         b_copy(da, 3).wait_recv()
-        x_copy(da, 2).start()
+        start(x_copy, da, 2)
 
     def find_tiles():
         row = lax.broadcasted_iota(jnp.int32, (TILES, TILES), 0)
@@ -218,16 +211,18 @@
         tile = lax.broadcasted_iota(jnp.int32, (TILES, SLOTS), 0)
         slot = lax.broadcasted_iota(jnp.int32, (TILES, SLOTS), 1)
         tab_row[...] = jnp.sum(jnp.where(place == slot, tile, 0), axis=0, keepdims=True)
-        move = pltpu.make_async_copy(tab_row, tab, in_s.at[0])
+        move = pltpu.make_async_copy(tab_row, tab, in_s.at[len(inputs)])
         move.start()
         return move
 
     def transpose_tiles(first, count):
-        def body(t, _):
-            wt[t] = w[t].T
+        def body(k, _):
+            for n in range(4):
+                t = first + 4 * k + n
+                wt[t] = w[t].T
             return 0
 
-        lax.fori_loop(first, first + count, body, 0)
+        lax.fori_loop(0, count // 4, body, 0)
 
     def tile_row(entries):
         tiles = [tab[0, i] for i in entries]
@@ -288,13 +283,14 @@
     z_start()
     a_start()
     b_start(0)
-    x_copy(0, 0).start()
+    start(x_copy, 0, 0)
     acc[...] = jnp.zeros_like(acc)
     deg[...] = jnp.zeros_like(deg)
-    for load in loads:
+    loads[0].wait()
+    found = find_tiles()
+    for load in loads[1:]:
         load.wait()
     gs[0, 0] = feat[0:2]
-    found = find_tiles()
     self_product()
     transpose_tiles(0, 12)
     found.wait()
@@ -308,7 +304,6 @@
     b_mid(0)
     z_pair(1)
     z_step(2, False)
-    z_first()
     local_tiles(0)
     z_step(2, True)
     a_end()
@@ -323,21 +318,24 @@
     z_step(4, False)
     transpose_tiles(40, 8)
     sub_pairs(0, 0)
+    drain(52)
     z_step(4, True)
     b_mid(2)
     b_end(1)
     b_end(3)
     z_pair(4)
     z_step(5, False)
-    transpose_tiles(48, 6)
+    transpose_tiles(48, 4)
     sub_pairs(0, 2)
+    drain(52)
     z_step(5, True)
     b_end(2)
     z_pair(5)
     sub_pairs(1, 0)
     z_step(6, False)
     sub_pairs(1, 2)
-    transpose_tiles(54, 6)
+    transpose_tiles(52, 8)
+    drain(52)
     local_tiles(4)
     z_step(6, True)
     z_pair(6)
@@ -371,26 +369,21 @@
     def k_copy(up_way, d, q):
         out_buf, in_buf, send, recv = (su, ru, ku_s, ku_r) if up_way else (sd, rd, kd_s, kd_r)
         h, rows = rows_of(q)
-        slot, device = d - 1, up if up_way else dn
-        if SKIP_B and is_far(up_way, q) and d == 2:
-            slot, device = 0, up2 if up_way else dn2
-        if SKIP_B and is_far(up_way, q) and d == 1:
-            slot = 1
         return copy(
-            out_buf.at[d - 1, h, rows], in_buf.at[slot, h, rows], send.at[slot, q], recv.at[slot, q], device
+            out_buf.at[d - 1, h, rows], in_buf.at[d - 1, h, rows], send.at[d - 1, q], recv.at[d - 1, q],
+            up if up_way else dn,
         )
 
     def k_send(up_way, d, q):
         out_buf, in_buf, part = (su, ru, pu) if up_way else (sd, rd, pd)
         h, rows = rows_of(q)
-        far = is_far(up_way, q)
         owner = wrap(c + d if up_way else c - d, NZ)
         value = only(rclu_ref[0, owner] == h, part[d - 1, rows])
-        if (SKIP_B < d < HALF) if far else d < HALF - 1:
+        if has(up_way, d + 1, q):
             k_copy(up_way, d + 1, q).wait_recv()
             value = value + in_buf[d, h, rows].astype(F32)
         out_buf[d - 1, h, rows] = value.astype(BF)
-        k_copy(up_way, d, q).start()
+        start(k_copy, up_way, d, q)
 
     def k_step(d, far):
         for q in range(PER):
@@ -399,21 +392,18 @@
 
     def z_partials(d):
         pu[d - 1] = partial(N_SUB + wrap(c + d, NZ))
-        pd[d - 1] = partial(N_SUB + wrap(c - d, NZ))
+        pd[d - 1] = pu[d - 1] if d == HALF else partial(N_SUB + wrap(c - d, NZ))
 
     def kx_copy(da, db):
         return copy(sb.at[da, db], rb.at[da, db], kx_s.at[da, db], kx_r.at[da, db], sib)
 
     def x_send(da):
-        def body(db, _):
+        for db in (2, 1, 3, 0):
             p = other_index(da, db)
             value = partial(p)
             for h in (0, 1):
                 sb[da, db, h] = only(rsub_ref[0, p] == h, value).astype(BF)
-            kx_copy(da, db).start()
-            return 0
-
-        lax.fori_loop(0, RING, body, 0)
+            start(kx_copy, da, db)
 
     def kb_copy(da, k):
         source, target, device = (
@@ -444,21 +434,29 @@
     def b_far(da):
         v0, v1 = chip_sum(da, 2)
         sbh[da, 0] = v0.astype(BF)
-        kb_copy(da, 2).start()
+        start(kb_copy, da, 2)
         sbh[da, 1] = v1.astype(BF)
-        kb_copy(da, 3).start()
-
-    def b_near(da):
+        start(kb_copy, da, 3)
+
+    def b_near(da, db=None):
+        if db != 3:
+            b_near_1(da)
+        if db != 1:
+            b_near_3(da)
+
+    def b_near_1(da):
         v0, v1 = chip_sum(da, 1)
         sbp[da, 0, 1] = v1.astype(BF)
         kb_copy(da, 2).wait_recv()
         sbp[da, 0, 0] = (v0 + rbh[da, 0].astype(F32)).astype(BF)
-        kb_copy(da, 0).start()
+        start(kb_copy, da, 0)
+
+    def b_near_3(da):
         v0, v1 = chip_sum(da, 3)
         sbp[da, 1, 0] = v0.astype(BF)
         kb_copy(da, 3).wait_recv()
         sbp[da, 1, 1] = (v1 + rbh[da, 1].astype(F32)).astype(BF)
-        kb_copy(da, 1).start()
+        start(kb_copy, da, 1)
 
     def row_sum(da):
         v = chip_sum(da, 0)
@@ -469,127 +467,119 @@
     def a_far():
         v = row_sum(2)
         sah[0] = v[0].astype(BF)
-        ka_copy(2).start()
+        start(ka_copy, 2)
         sah[1] = v[1].astype(BF)
-        ka_copy(3).start()
+        start(ka_copy, 3)
 
     def a_near():
         v = row_sum(1)
         ka_copy(2).wait_recv()
         sap[0, 0] = (v[0] + rah[0].astype(F32)).astype(BF)
         sap[0, 1] = v[1].astype(BF)
-        ka_copy(0).start()
+        start(ka_copy, 0)
         v = row_sum(3)
         ka_copy(3).wait_recv()
         sap[1, 0] = v[0].astype(BF)
         sap[1, 1] = (v[1] + rah[1].astype(F32)).astype(BF)
-        ka_copy(1).start()
-
-    def add_local():
-        def body(k, _):
-            i = REMOTE + k
-            value = partial(i)
-            j = src_ref[0, tab[0, i]]
-            for n in range(OWN):
-                gself[n] += only(j == n, value)
-            return 0
-
-        lax.fori_loop(0, LOCAL, body, 0)
+        start(ka_copy, 1)
+
+    def add_local(first):
+        entries = [REMOTE + first + k for k in range(4)]
+        values = [partial(i) for i in entries]
+        blocks = [src_ref[0, tab[0, i]] for i in entries]
+        for n in range(OWN):
+            gself[n] += sum(only(j == n, value) for j, value in zip(blocks, values))
+
+    def add_own():
         value = partial(N_SUB + c)
         for h in (0, 1):
             gself[h] += only(rclu_ref[0, c] == h, value)
+
+    def grad_self():
+        gself[...] = dot_nt(grad_pre, ws[...]).reshape(OWN, BLK, D)
 
     z_partials(HALF)
     k_step(HALF, True)
     z_partials(7)
     k_step(7, False)
-    z_partials(1)
-    if SKIP_B:
-        k_step(1, True)
     x_send(2)
+    x_send(1)
     z_partials(6)
-
     k_step(7, True)
-    x_send(1)
+    x_send(3)
     k_step(6, False)
-    x_send(3)
+    x_send(0)
     z_partials(5)
-
     k_step(6, True)
     b_far(2)
+    drain(60)
     k_step(5, False)
-    x_send(0)
+    b_far(1)
     z_partials(4)
-
     k_step(5, True)
-    b_far(1)
     b_far(3)
+    b_far(0)
+    drain(60)
     k_step(4, False)
-    b_far(0)
+    b_near(2)
     z_partials(3)
-
     k_step(4, True)
-    b_near(2)
+    b_near(1)
+    drain(56)
     k_step(3, False)
-    b_near(1)
+    b_near(3)
     z_partials(2)
-
     k_step(3, True)
-    b_near(3)
+    a_far()
+    drain(48)
     k_step(2, False)
     b_near(0)
-
+    z_partials(1)
     k_step(2, True)
-    a_far()
+    grad_self()
+    add_local(0)
+    drain(40)
     k_step(1, False)
     a_near()
-    if not SKIP_B:
-        k_step(1, True)
-    gself[...] = dot_nt(grad_pre, ws[...]).reshape(OWN, BLK, D)
-    add_local()
+    add_local(4)
+    k_step(1, True)
+    add_local(8)
+    add_own()
+    drain(24)
 
     v = row_sum(0)
     ka_copy(0).wait_recv()
     ka_copy(1).wait_recv()
+    puts = []
+
+    def put(h, rows, k):
+        puts.append(pltpu.make_async_copy(out.at[h, rows], out_hbm.at[h, rows], in_s.at[k]))
+        puts[-1].start()
+
     out[2] = gself[2].astype(BF)
+    put(2, pl.ds(0, BLK), CHUNKS)
     for q in range(CHUNKS):
         h, rows = rows_of(q)
         total = gself[h, rows] + v[h][q % PER * ROWS : (q % PER + 1) * ROWS]
         total = total + rap[0, h, rows].astype(F32) + rap[1, h, rows].astype(F32)
         for up_way, buf in ((True, ru), (False, rd)):
-            far = SKIP_B and is_far(up_way, q)
-            if far:
-                k_copy(up_way, 1, q).wait_recv()
-                total = total + buf[1, h, rows].astype(F32)
-            k_copy(up_way, 2 if far else 1, q).wait_recv()
+            k_copy(up_way, 1, q).wait_recv()
             total = total + buf[0, h, rows].astype(F32)
         out[h, rows] = total.astype(BF)
-
-    for d in range(1, HALF + 1):
-        for q in range(CHUNKS):
-            for up_way in (True, False):
-                if has(up_way, d, q):
-                    z_copy(up_way, d, q).wait_send()
-                    k_copy(up_way, d, q).wait_send()
-    for k in range(4):
-        a_copy(k).wait_send()
-        ka_copy(k).wait_send()
-    for da in range(RING):
-        for k in range(4):
-            b_copy(da, k).wait_send()
-            kb_copy(da, k).wait_send()
-        for db in range(RING):
-            x_copy(da, db).wait_send()
-            kx_copy(da, db).wait_send()
+        put(h, rows, q)
+
+    drain(0)
+    for cp in puts:
+        cp.wait()
 
 
 def shards(
     features, grad_out, w_self, w_neigh, bias, tile_dst, tile_src, tile_weight, recv_sub, recv_cluster
 ):
     blk = (BLK, D)
-    vmem = pl.BlockSpec(memory_space=pltpu.VMEM)
     sems = [(HALF, CHUNKS)] * 4 + [(4,)] * 2 + [(RING, 4)] * 2 + [(RING, RING)] * 2
     scratch = [
+        pltpu.VMEM((OWN,) + blk, BF),
         pltpu.SMEM((1, TILES), jnp.int32),
         pltpu.SMEM((1, TILES), jnp.int32),
         pltpu.SMEM((1, N_SUB), jnp.int32),
@@ -630,13 +620,13 @@
         pltpu.VMEM((2,) + blk, BF),
         pltpu.VMEM((2, 2) + blk, BF),
         pltpu.VMEM((2,) + blk, BF),
-        pltpu.SemaphoreType.DMA((11,)),
+        pltpu.SemaphoreType.DMA((12,)),
     ] + [pltpu.SemaphoreType.DMA(shape) for shape in sems + sems]
     result = pl.pallas_call(
         kernel,
         out_shape=jax.ShapeDtypeStruct((OWN,) + blk, BF),
         in_specs=[pl.BlockSpec(memory_space=pl.ANY)] * 10,
-        out_specs=vmem,
+        out_specs=pl.BlockSpec(memory_space=pl.ANY),
         scratch_shapes=scratch,
         compiler_params=pltpu.CompilerParams(
             collective_id=0, has_side_effects=True, vmem_limit_bytes=VMEM_BYTES

time: 79 us -> 75.7 us (0.958)
  Pallas kernels: 77 us -> 73.9 us
    pallas_call x1, Pallas kernels: 77 us -> 73.9 us  [shards(): pl.pallas_call(kernel, out_shape=jax.ShapeDtypeStruct((OWN,) + blk, BF),...]
where the time goes in v3:
time: 75.7 us; the launch traced here: 75.5 us
  Pallas kernels  73.9 us (98%)
  local copies, waits for them, and re-layouts  1.62 us (2%)
    pallas_call x1, Pallas kernels, shards(): pl.pallas_call(kernel, out_shape=jax.ShapeDtypeStruct((OWN,) + blk, BF),...  73.9 us
    unnamed x1, local copies, waits for them, and re-layouts  1.62 us

profile of v3, /device:TPU:24, one launch (start us, length us, event | category | flops | bytes accessed | tf_op | source)
XLA Modules:
  0.0 75.5 jit_solution(3495352507635600020)
XLA Ops:
  0.0 73.9 %sage_layer.1 = bf16[3,128,256]{2,1,0:T(8,128)(2,1)} custom-call(s32[1,60]{1,0:T(1,128)} %bitcast.8, s32[1,60]{1,0:T(1,128)} %bitcast.9, s32[1,32]{1,0:T(1,128)} %rsub_hbm.1, s32[1,16]{1,0:T(1,128)} %rclu_hbm.1, bf16[3,128,256]{2,1,0:T(8,128)(2,1)} %bitcast.6, bf16[384,256]{1,0:T(8,128)(2,1)} %gout_hbm.1, bf16[256,256]{1,0:T(8,128)(2,1)} %ws_hbm.1, ...), custom_call_target="tpu_custom_call" | custom-call | tf_op jit(solution)/shard_map/sage_layer/pallas_call | solution.py:625
  73.9 1.6 %copy.12 = bf16[384,256]{1,0:T(8,128)(2,1)} copy(bf16[384,256]{1,0:T(8,128)(2,1)} %bitcast.5) | data formatting | bytes 393216

commit v4 on v3

--- a/solution.py
+++ b/solution.py
@@ -1,4 +1,4 @@
-import functools
+import itertools
 
 import jax
 import jax.numpy as jnp
@@ -21,6 +21,7 @@
 REMOTE = N_SUB + NZ
 LOCAL = TILES - REMOTE
 SLOTS = 128
+POOL = 40
 CHUNKS = 4
 PER = CHUNKS // 2
 ROWS = BLK // PER
@@ -45,8 +46,7 @@
     pu, pd, su, sd, ru, rd,
     sb, rb, sbp, sbh, rbp, rbh, sap, sah, rap, rah,
     in_s,
-    zu_s, zu_r, zd_s, zd_r, a_s, a_r, b_s, b_r, x_s, x_r,
-    ku_s, ku_r, kd_s, kd_r, ka_s, ka_r, kb_s, kb_r, kx_s, kx_r,
+    pool, zu_r, zd_r, a_r, b_r, x_r, ku_r, kd_r, ka_r, kb_r, kx_r,
 ):
     c = lax.axis_index("cluster")
     s = lax.axis_index("sub")
@@ -71,22 +71,25 @@
     bm = (c, at(0, -1, core))
     sib = (c, at(0, 0, 1 - core))
 
-    def copy(source, target, send, recv, device):
+    def copy(source, target, recv, device, lane=0):
         return pltpu.make_async_remote_copy(
-            src_ref=source, dst_ref=target, send_sem=send, recv_sem=recv,
+            src_ref=source, dst_ref=target, send_sem=pool.at[lane], recv_sem=recv,
             device_id=device, device_id_type=MESH,
         )
 
     sent = []
+    lanes = itertools.cycle(range(POOL))
 
     def start(make, *args):
-        make(*args).start()
-        sent.append((make, args))
+        drain(POOL - 1)
+        lane = next(lanes)
+        make(*args, lane=lane).start()
+        sent.append((make, args, lane))
 
     def drain(keep):
         while len(sent) > keep:
-            make, args = sent.pop(0)
-            make(*args).wait_send()
+            make, args, lane = sent.pop(0)
+            make(*args, lane=lane).wait_send()
 
     def same_index(da, db):
         return at(-da, -db, core)
@@ -116,12 +119,12 @@
     def has(up_way, d, q):
         return d < HALF or (d == HALF and is_far(up_way, q))
 
-    def z_copy(up_way, d, q):
-        buf, send, recv = (zu, zu_s, zu_r) if up_way else (zd, zd_s, zd_r)
+    def z_copy(up_way, d, q, lane=0):
+        buf, recv = (zu, zu_r) if up_way else (zd, zd_r)
         h, rows = rows_of(q)
         source = buf.at[d - 2, h, rows] if d > 1 else feat_hbm.at[h, rows]
         device = up if up_way else dn
-        return copy(source, buf.at[d - 1, h, rows], send.at[d - 1, q], recv.at[d - 1, q], device)
+        return copy(source, buf.at[d - 1, h, rows], recv.at[d - 1, q], device, lane)
 
     def z_start():
         for far in (True, False):
@@ -140,29 +143,27 @@
 
     own = feat_hbm.at[pl.ds(0, 2)]
 
-    def a_copy(k):
+    def a_copy(k, lane=0):
         source, target, device = (
             (own, gs.at[1, 0], ap),
             (own, gs.at[3, 0], am),
             (gs.at[1, 0, 0], gs.at[2, 0, 0], ap),
             (gs.at[3, 0, 1], gs.at[2, 0, 1], am),
         )[k]
-        return copy(source, target, a_s.at[k], a_r.at[k], device)
-
-    def b_copy(da, k):
+        return copy(source, target, a_r.at[min(k, 2)], device, lane)
+
+    def b_copy(da, k, lane=0):
         source, target, device = (
             (gs.at[da, 0] if da else own, gs.at[da, 1], bp),
             (gs.at[da, 0] if da else own, gs.at[da, 3], bm),
             (gs.at[da, 1, 0], gs.at[da, 2, 0], bp),
             (gs.at[da, 3, 1], gs.at[da, 2, 1], bm),
         )[k]
-        return copy(source, target, b_s.at[da, k], b_r.at[da, k], device)
-
-    def x_copy(da, db):
-        source = gs.at[da, db]
-        if da == 0 and isinstance(db, int) and db == 0:
-            source = own
-        return copy(source, gb.at[da, db], x_s.at[da, db], x_r.at[da, db], sib)
+        return copy(source, target, b_r.at[da, min(k, 2)], device, lane)
+
+    def x_copy(da, db, lane=0):
+        source = own if (da, db) == (0, 0) else gs.at[da, db]
+        return copy(source, gb.at[da, db], x_r.at[da], sib, lane)
 
     def a_start():
         start(a_copy, 0)
@@ -178,8 +179,7 @@
             start(x_copy, da, 0)
 
     def a_end():
-        a_copy(2).wait_recv()
-        a_copy(3).wait_recv()
+        copy(gs.at[2, 0], gs.at[2, 0], a_r.at[2], ap).wait_recv()
         b_start(2)
         start(x_copy, 2, 0)
 
@@ -196,8 +196,7 @@
         start(x_copy, da, 3)
 
     def b_end(da):
-        b_copy(da, 2).wait_recv()
-        b_copy(da, 3).wait_recv()
+        copy(gs.at[da, 2], gs.at[da, 2], b_r.at[da, 2], bp).wait_recv()
         start(x_copy, da, 2)
 
     def find_tiles():
@@ -265,8 +264,9 @@
 
     def sub_pairs(da, first):
         entries, blocks = [], []
+        if first == 0:
+            copy(gb.at[da], gb.at[da], x_r.at[da], sib).wait_recv()
         for db in (first, first + 1):
-            x_copy(da, db).wait_recv()
             for p, buf in ((same_index(da, db), gs), (other_index(da, db), gb)):
                 entries.append(p)
                 blocks.append(jnp.where(rsub_ref[0, p] == 0, buf[da, db, 0], buf[da, db, 1]))
@@ -318,7 +318,7 @@
     z_step(4, False)
     transpose_tiles(40, 8)
     sub_pairs(0, 0)
-    drain(52)
+    drain(32)
     z_step(4, True)
     b_mid(2)
     b_end(1)
@@ -327,7 +327,7 @@
     z_step(5, False)
     transpose_tiles(48, 4)
     sub_pairs(0, 2)
-    drain(52)
+    drain(32)
     z_step(5, True)
     b_end(2)
     z_pair(5)
@@ -335,7 +335,7 @@
     z_step(6, False)
     sub_pairs(1, 2)
     transpose_tiles(52, 8)
-    drain(52)
+    drain(32)
     local_tiles(4)
     z_step(6, True)
     z_pair(6)
@@ -366,12 +366,12 @@
     def only(keep, value):
         return jnp.where(keep, value, jnp.zeros_like(value))
 
-    def k_copy(up_way, d, q):
-        out_buf, in_buf, send, recv = (su, ru, ku_s, ku_r) if up_way else (sd, rd, kd_s, kd_r)
+    def k_copy(up_way, d, q, lane=0):
+        out_buf, in_buf, recv = (su, ru, ku_r) if up_way else (sd, rd, kd_r)
         h, rows = rows_of(q)
         return copy(
-            out_buf.at[d - 1, h, rows], in_buf.at[d - 1, h, rows], send.at[d - 1, q], recv.at[d - 1, q],
-            up if up_way else dn,
+            out_buf.at[d - 1, h, rows], in_buf.at[d - 1, h, rows], recv.at[d - 1, q],
+            up if up_way else dn, lane,
         )
 
     def k_send(up_way, d, q):
@@ -394,8 +394,8 @@
         pu[d - 1] = partial(N_SUB + wrap(c + d, NZ))
         pd[d - 1] = pu[d - 1] if d == HALF else partial(N_SUB + wrap(c - d, NZ))
 
-    def kx_copy(da, db):
-        return copy(sb.at[da, db], rb.at[da, db], kx_s.at[da, db], kx_r.at[da, db], sib)
+    def kx_copy(da, db, lane=0):
+        return copy(sb.at[da, db], rb.at[da, db], kx_r.at[da], sib, lane)
 
     def x_send(da):
         for db in (2, 1, 3, 0):
@@ -405,28 +405,29 @@
                 sb[da, db, h] = only(rsub_ref[0, p] == h, value).astype(BF)
             start(kx_copy, da, db)
 
-    def kb_copy(da, k):
+    def kb_copy(da, k, lane=0):
         source, target, device = (
             (sbp.at[da, 0], rbp.at[da, 0], bm),
             (sbp.at[da, 1], rbp.at[da, 1], bp),
             (sbh.at[da, 0], rbh.at[da, 0], bm),
             (sbh.at[da, 1], rbh.at[da, 1], bp),
         )[k]
-        return copy(source, target, kb_s.at[da, k], kb_r.at[da, k], device)
-
-    def ka_copy(k):
+        return copy(source, target, kb_r.at[da, k], device, lane)
+
+    def ka_copy(k, lane=0):
         source, target, device = (
             (sap.at[0], rap.at[0], am),
             (sap.at[1], rap.at[1], ap),
             (sah.at[0], rah.at[0], am),
             (sah.at[1], rah.at[1], ap),
         )[k]
-        return copy(source, target, ka_s.at[k], ka_r.at[k], device)
+        return copy(source, target, ka_r.at[k], device, lane)
 
     def chip_sum(da, db):
         p = same_index(da, db)
         value = partial(p)
-        kx_copy(da, db).wait_recv()
+        if db == 2:
+            copy(rb.at[da], rb.at[da], kx_r.at[da], sib).wait_recv()
         return [
             only(rsub_ref[0, p] == h, value) + rb[da, db, h].astype(F32) for h in (0, 1)
         ]
@@ -512,40 +513,40 @@
     z_partials(5)
     k_step(6, True)
     b_far(2)
-    drain(60)
+    drain(32)
     k_step(5, False)
     b_far(1)
     z_partials(4)
     k_step(5, True)
     b_far(3)
     b_far(0)
-    drain(60)
+    drain(32)
     k_step(4, False)
     b_near(2)
     z_partials(3)
     k_step(4, True)
     b_near(1)
-    drain(56)
+    drain(32)
     k_step(3, False)
     b_near(3)
     z_partials(2)
     k_step(3, True)
     a_far()
-    drain(48)
+    drain(32)
     k_step(2, False)
     b_near(0)
     z_partials(1)
     k_step(2, True)
     grad_self()
     add_local(0)
-    drain(40)
+    drain(28)
     k_step(1, False)
     a_near()
     add_local(4)
     k_step(1, True)
     add_local(8)
     add_own()
-    drain(24)
+    drain(16)
 
     v = row_sum(0)
     ka_copy(0).wait_recv()
@@ -577,7 +578,8 @@
     features, grad_out, w_self, w_neigh, bias, tile_dst, tile_src, tile_weight, recv_sub, recv_cluster
 ):
     blk = (BLK, D)
-    sems = [(HALF, CHUNKS)] * 4 + [(4,)] * 2 + [(RING, 4)] * 2 + [(RING, RING)] * 2
+    ring_sems = [(HALF, CHUNKS)] * 2
+    sems = [(POOL,)] + ring_sems + [(3,), (RING, 3), (RING,)] + ring_sems + [(4,), (RING, 4), (RING,)]
     scratch = [
         pltpu.VMEM((OWN,) + blk, BF),
         pltpu.SMEM((1, TILES), jnp.int32),
@@ -621,7 +623,7 @@
         pltpu.VMEM((2, 2) + blk, BF),
         pltpu.VMEM((2,) + blk, BF),
         pltpu.SemaphoreType.DMA((12,)),
-    ] + [pltpu.SemaphoreType.DMA(shape) for shape in sems + sems]
+    ] + [pltpu.SemaphoreType.DMA(shape) for shape in sems]
     result = pl.pallas_call(
         kernel,
         out_shape=jax.ShapeDtypeStruct((OWN,) + blk, BF),

time: 75.7 us -> 74 us (0.978)
  Pallas kernels: 73.9 us -> 72.2 us
    pallas_call x1, Pallas kernels: 73.9 us -> 72.2 us  [shards(): pl.pallas_call(kernel, out_shape=jax.ShapeDtypeStruct((OWN,) + blk, BF),...]
where the time goes in v4:
time: 74 us; the launch traced here: 73.9 us
  Pallas kernels  72.2 us (98%)
  local copies, waits for them, and re-layouts  1.62 us (2%)
    pallas_call x1, Pallas kernels, shards(): pl.pallas_call(kernel, out_shape=jax.ShapeDtypeStruct((OWN,) + blk, BF),...  72.2 us
    unnamed x1, local copies, waits for them, and re-layouts  1.62 us

profile of v4, /device:TPU:24, one launch (start us, length us, event | category | flops | bytes accessed | tf_op | source)
XLA Modules:
  0.0 73.9 jit_solution(7881213178595209021)
XLA Ops:
  0.0 72.2 %sage_layer.1 = bf16[3,128,256]{2,1,0:T(8,128)(2,1)} custom-call(s32[1,60]{1,0:T(1,128)} %bitcast.8, s32[1,60]{1,0:T(1,128)} %bitcast.9, s32[1,32]{1,0:T(1,128)} %rsub_hbm.1, s32[1,16]{1,0:T(1,128)} %rclu_hbm.1, bf16[3,128,256]{2,1,0:T(8,128)(2,1)} %bitcast.6, bf16[384,256]{1,0:T(8,128)(2,1)} %gout_hbm.1, bf16[256,256]{1,0:T(8,128)(2,1)} %ws_hbm.1, ...), custom_call_target="tpu_custom_call" | custom-call | tf_op jit(solution)/shard_map/sage_layer/pallas_call | solution.py:627
  72.2 1.6 %copy.12 = bf16[384,256]{1,0:T(8,128)(2,1)} copy(bf16[384,256]{1,0:T(8,128)(2,1)} %bitcast.5) | data formatting | bytes 393216

commit v5 on v4

--- a/solution.py
+++ b/solution.py
@@ -46,7 +46,7 @@
     pu, pd, su, sd, ru, rd,
     sb, rb, sbp, sbh, rbp, rbh, sap, sah, rap, rah,
     in_s,
-    pool, zu_r, zd_r, a_r, b_r, x_r, ku_r, kd_r, ka_r, kb_r, kx_r,
+    pool, zu_r, zd_r, a_r, b_r, x_r, k_r, ka_r, kb_r, kx_r,
 ):
     c = lax.axis_index("cluster")
     s = lax.axis_index("sub")
@@ -366,11 +366,16 @@
     def only(keep, value):
         return jnp.where(keep, value, jnp.zeros_like(value))
 
+    def k_recv(up_way, d, q):
+        if d == 7 and is_far(up_way, q):
+            return k_r.at[q]
+        return (zd_r if up_way else zu_r).at[d - 1, q]
+
     def k_copy(up_way, d, q, lane=0):
-        out_buf, in_buf, recv = (su, ru, ku_r) if up_way else (sd, rd, kd_r)
+        out_buf, in_buf = (su, ru) if up_way else (sd, rd)
         h, rows = rows_of(q)
         return copy(
-            out_buf.at[d - 1, h, rows], in_buf.at[d - 1, h, rows], recv.at[d - 1, q],
+            out_buf.at[d - 1, h, rows], in_buf.at[d - 1, h, rows], k_recv(up_way, d, q),
             up if up_way else dn, lane,
         )
 
@@ -579,7 +584,7 @@
 ):
     blk = (BLK, D)
     ring_sems = [(HALF, CHUNKS)] * 2
-    sems = [(POOL,)] + ring_sems + [(3,), (RING, 3), (RING,)] + ring_sems + [(4,), (RING, 4), (RING,)]
+    sems = [(POOL,)] + ring_sems + [(3,), (RING, 3), (RING,), (CHUNKS,), (4,), (RING, 4), (RING,)]
     scratch = [
         pltpu.VMEM((OWN,) + blk, BF),
         pltpu.SMEM((1, TILES), jnp.int32),

time: 74 us -> 73.5 us (level)
  no operation moved by 1% of the time
where the time goes in v5:
time: 73.5 us; the launch traced here: 73.3 us
  Pallas kernels  71.7 us (98%)
  local copies, waits for them, and re-layouts  1.62 us (2%)
    pallas_call x1, Pallas kernels, shards(): pl.pallas_call(kernel, out_shape=jax.ShapeDtypeStruct((OWN,) + blk, BF),...  71.7 us
    unnamed x1, local copies, waits for them, and re-layouts  1.62 us

profile of v5, /device:TPU:24, one launch (start us, length us, event | category | flops | bytes accessed | tf_op | source)
XLA Modules:
  0.0 73.3 jit_solution(17599320003343179821)
XLA Ops:
  0.0 71.7 %sage_layer.1 = bf16[3,128,256]{2,1,0:T(8,128)(2,1)} custom-call(s32[1,60]{1,0:T(1,128)} %bitcast.8, s32[1,60]{1,0:T(1,128)} %bitcast.9, s32[1,32]{1,0:T(1,128)} %rsub_hbm.1, s32[1,16]{1,0:T(1,128)} %rclu_hbm.1, bf16[3,128,256]{2,1,0:T(8,128)(2,1)} %bitcast.6, bf16[384,256]{1,0:T(8,128)(2,1)} %gout_hbm.1, bf16[256,256]{1,0:T(8,128)(2,1)} %ws_hbm.1, ...), custom_call_target="tpu_custom_call" | custom-call | tf_op jit(solution)/shard_map/sage_layer/pallas_call | solution.py:632
  71.7 1.6 %copy.12 = bf16[384,256]{1,0:T(8,128)(2,1)} copy(bf16[384,256]{1,0:T(8,128)(2,1)} %bitcast.5) | data formatting | bytes 393216
